TPU v7x, 32 devices: a whole 2x2x4 slice. The times are simulated.
32 devices in a mesh: wide: 16 (over z, x, core), narrow: 2 (over y).
Axes of the slice: x: 2, y: 2, z: 4, core: 2. Of those that a mesh axis runs over, the one named last changes fastest.
Arguments:
- tokens: bfloat16 [32768, 768], P(('wide', 'narrow')), may hold values from -6 to 6
- cotangent: bfloat16 [32768, 768], P(('wide', 'narrow')), may hold values from -6 to 6
- lengths: int32 [32], P(('wide', 'narrow')), may hold values from 512 to 1024, as said below
- ln1_gain: bfloat16 [768], P(('wide', 'narrow')), may hold values from 0.099609375 to 1.8984375
- ln1_shift: bfloat16 [768], P(('wide', 'narrow')), may hold values from -3 to 3
- qkv_weight: bfloat16 [768, 2304], P(('wide', 'narrow')), may hold values from -0.21875 to 0.21875
- qkv_bias: bfloat16 [2304], P(('wide', 'narrow')), may hold values from -3 to 3
- out_weight: bfloat16 [768, 768], P(('wide', 'narrow')), may hold values from -1.25 to 1.25
- out_bias: bfloat16 [768], P(('wide', 'narrow')), may hold values from -3 to 3
- ln2_gain: bfloat16 [768], P(('wide', 'narrow')), may hold values from 0.099609375 to 1.8984375
- ln2_shift: bfloat16 [768], P(('wide', 'narrow')), may hold values from -3 to 3
- up_weight: bfloat16 [768, 3072], P(('wide', 'narrow')), may hold values from -0.21875 to 0.21875
- up_bias: bfloat16 [3072], P(('wide', 'narrow')), may hold values from -3 to 3
- down_weight: bfloat16 [3072, 768], P(('wide', 'narrow')), may hold values from -0.109375 to 0.109375
- down_bias: bfloat16 [768], P(('wide', 'narrow')), may hold values from -3 to 3
Outputs:
- mixed: bfloat16 [32768, 768], P(('wide', 'narrow'))
- grad_tokens: bfloat16 [32768, 768], P(('wide', 'narrow'))
- grad_ln1_gain: float32 [768], P(('wide', 'narrow'))
- grad_ln1_shift: float32 [768], P(('wide', 'narrow'))
- grad_qkv_weight: float32 [768, 2304], P(('wide', 'narrow'))
- grad_qkv_bias: float32 [2304], P(('wide', 'narrow'))
- grad_out_weight: float32 [768, 768], P(('wide', 'narrow'))
- grad_out_bias: float32 [768], P(('wide', 'narrow'))
- grad_ln2_gain: float32 [768], P(('wide', 'narrow'))
- grad_ln2_shift: float32 [768], P(('wide', 'narrow'))
- grad_up_weight: float32 [768, 3072], P(('wide', 'narrow'))
- grad_up_bias: float32 [3072], P(('wide', 'narrow'))
- grad_down_weight: float32 [3072, 768], P(('wide', 'narrow'))
- grad_down_bias: float32 [768], P(('wide', 'narrow'))
Inputs may be any that keep to these rules, and one draw needn't show every extreme that they name: `lengths`: each value is 1024 or 512; 1024 is taken by some device in every draw.
All inputs are finite; a program needn't handle non-finite values.
Results may differ from a plain program's by a relative error of at most 0.012.
Values may be sent and summed in bfloat16 or wider, within the bound.
A program may use at most 192 MiB of HBM per device.

v0:
```python
import jax
import jax.numpy as jnp
from jax import lax
from jax.sharding import PartitionSpec as P

D = 768
HEADS = 12
HEAD = 64


def norm_parts(values):
    average = jnp.mean(values, axis=-1, keepdims=True)
    centered = values - average
    inverse = lax.rsqrt(jnp.mean(centered * centered, axis=-1, keepdims=True) + 1e-05)
    return (centered * inverse, inverse)


def norm_back(grad_normed, normed, inverse):
    first_mean = jnp.mean(grad_normed, axis=-1, keepdims=True)
    second_mean = jnp.mean(grad_normed * normed, axis=-1, keepdims=True)
    return inverse * (grad_normed - first_mean - normed * second_mean)


def causal_mask(length):
    positions = jnp.arange(length, dtype=jnp.int32)
    return positions[:, None] >= positions[None, :]


def head_scores(query, key_rows):
    scores = jnp.einsum("qd,kd->qk", query, key_rows, preferred_element_type=jnp.float32) * 0.125
    return (scores, jnp.sqrt(scores * scores + 1.0))


def head_forward(parts):
    query, key_rows, value_rows = parts
    causal = causal_mask(query.shape[0])
    scores, magnitude = head_scores(query, key_rows)
    masked = jnp.where(causal, magnitude, -1e30)
    highest = jnp.max(masked, axis=1, keepdims=True)
    expon = jnp.where(causal, jnp.exp(masked - highest), 0.0)
    total = jnp.sum(expon, axis=1, keepdims=True)
    weights = (jnp.tanh(scores) * (expon / total)).astype(jnp.bfloat16)
    result = jnp.dot(weights, value_rows, preferred_element_type=jnp.float32)
    return (result, (highest + jnp.log(total))[:, 0])


def head_backward(parts):
    query, key_rows, value_rows, grad_out, log_norm = parts
    causal = causal_mask(query.shape[0])
    scores, magnitude = head_scores(query, key_rows)
    prob = jnp.where(causal, jnp.exp(magnitude - log_norm[:, None]), 0.0)
    slope = jnp.tanh(scores)
    weights = (slope * prob).astype(jnp.bfloat16)
    grad_weights = jnp.einsum("qd,kd->qk", grad_out, value_rows, preferred_element_type=jnp.float32)
    grad_value = jnp.einsum("qk,qd->kd", weights, grad_out, preferred_element_type=jnp.float32)
    grad_prob = grad_weights * slope
    grad_mag = prob * (grad_prob - jnp.sum(grad_prob * prob, axis=1, keepdims=True))
    grad_scores = grad_weights * prob * (1.0 - slope * slope) + grad_mag * scores / magnitude
    grad_scores = jnp.where(causal, grad_scores, 0.0).astype(jnp.bfloat16)
    grad_query = (
        jnp.einsum("qk,kd->qd", grad_scores, key_rows, preferred_element_type=jnp.float32) * 0.125
    )
    grad_key = (
        jnp.einsum("qk,qd->kd", grad_scores, query, preferred_element_type=jnp.float32) * 0.125
    )
    return (grad_query, grad_key, grad_value)


def column_sum(values):
    return jnp.sum(values, axis=0, dtype=jnp.float32)


def weight_grad(left, right):
    return jnp.einsum("rd,rf->df", left, right, preferred_element_type=jnp.float32)


def shards(
    tokens,
    cotangent,
    lengths,
    ln1_gain,
    ln1_shift,
    qkv_weight,
    qkv_bias,
    out_weight,
    out_bias,
    ln2_gain,
    ln2_shift,
    up_weight,
    up_bias,
    down_weight,
    down_bias,
):
    length = tokens.shape[0]
    attn_full = (
        lax.all_gather(ln1_gain, ("wide", "narrow"), axis=0, tiled=True),
        lax.all_gather(ln1_shift, ("wide", "narrow"), axis=0, tiled=True),
        lax.all_gather(qkv_weight, ("wide", "narrow"), axis=0, tiled=True),
        lax.all_gather(qkv_bias, ("wide", "narrow"), axis=0, tiled=True),
        lax.all_gather(out_weight, ("wide", "narrow"), axis=0, tiled=True),
        lax.all_gather(out_bias, ("wide", "narrow"), axis=0, tiled=True),
    )
    inputs = tokens.astype(jnp.float32)
    normed_one, inverse_one = norm_parts(inputs)
    gain_one = attn_full[0].astype(jnp.float32)
    hidden_one = (normed_one * gain_one + attn_full[1].astype(jnp.float32)).astype(jnp.bfloat16)
    qkv = (
        jnp.dot(hidden_one, attn_full[2], preferred_element_type=jnp.float32)
        + attn_full[3].astype(jnp.float32)
    ).astype(jnp.bfloat16)
    split = qkv.reshape(length, 3, HEADS, HEAD).transpose(1, 2, 0, 3)
    head_outs, log_norms = lax.map(head_forward, (split[0], split[1], split[2]))
    attended = head_outs.transpose(1, 0, 2).reshape(length, D).astype(jnp.bfloat16)
    middle = (
        inputs
        + jnp.dot(attended, attn_full[4], preferred_element_type=jnp.float32)
        + attn_full[5].astype(jnp.float32)
    )
    mlp_full = (
        lax.all_gather(ln2_gain, ("wide", "narrow"), axis=0, tiled=True),
        lax.all_gather(ln2_shift, ("wide", "narrow"), axis=0, tiled=True),
        lax.all_gather(up_weight, ("wide", "narrow"), axis=0, tiled=True),
        lax.all_gather(up_bias, ("wide", "narrow"), axis=0, tiled=True),
        lax.all_gather(down_weight, ("wide", "narrow"), axis=0, tiled=True),
        lax.all_gather(down_bias, ("wide", "narrow"), axis=0, tiled=True),
    )
    normed_two, inverse_two = norm_parts(middle)
    gain_two = mlp_full[0].astype(jnp.float32)
    hidden_two = (normed_two * gain_two + mlp_full[1].astype(jnp.float32)).astype(jnp.bfloat16)
    upward = jnp.dot(hidden_two, mlp_full[2], preferred_element_type=jnp.float32) + mlp_full[
        3
    ].astype(jnp.float32)
    activated, gelu_back = jax.vjp(lambda values: jax.nn.gelu(values, approximate=True), upward)
    activated = activated.astype(jnp.bfloat16)
    output = (
        middle
        + jnp.dot(activated, mlp_full[4], preferred_element_type=jnp.float32)
        + mlp_full[5].astype(jnp.float32)
    )
    mixed = output.astype(jnp.bfloat16)
    slots = jnp.arange(length, dtype=jnp.int32)
    live = (slots < lengths[0])[:, None]
    upstream = jnp.where(live, cotangent, jnp.zeros_like(cotangent))
    mlp_back = (
        lax.all_gather(ln2_gain, ("wide", "narrow"), axis=0, tiled=True),
        lax.all_gather(ln2_shift, ("wide", "narrow"), axis=0, tiled=True),
        lax.all_gather(up_weight, ("wide", "narrow"), axis=0, tiled=True),
        lax.all_gather(up_bias, ("wide", "narrow"), axis=0, tiled=True),
        lax.all_gather(down_weight, ("wide", "narrow"), axis=0, tiled=True),
        lax.all_gather(down_bias, ("wide", "narrow"), axis=0, tiled=True),
    )
    grad_down = weight_grad(activated, upstream)
    grad_down_bias = column_sum(upstream)
    grad_act = jnp.einsum("rd,fd->rf", upstream, mlp_back[4], preferred_element_type=jnp.float32)
    grad_up_rows = gelu_back(grad_act)[0].astype(jnp.bfloat16)
    grad_up = weight_grad(hidden_two, grad_up_rows)
    grad_up_bias = column_sum(grad_up_rows)
    grad_hidden_two = jnp.einsum(
        "rf,df->rd", grad_up_rows, mlp_back[2], preferred_element_type=jnp.float32
    )
    grad_gain_two = jnp.sum(grad_hidden_two * normed_two, axis=0)
    grad_shift_two = jnp.sum(grad_hidden_two, axis=0)
    grad_middle = upstream.astype(jnp.float32) + norm_back(
        grad_hidden_two * mlp_back[0].astype(jnp.float32), normed_two, inverse_two
    )
    mlp_shares = (
        lax.psum_scatter(grad_gain_two, ("wide", "narrow"), scatter_dimension=0, tiled=True),
        lax.psum_scatter(grad_shift_two, ("wide", "narrow"), scatter_dimension=0, tiled=True),
        lax.psum_scatter(grad_up, ("wide", "narrow"), scatter_dimension=0, tiled=True),
        lax.psum_scatter(grad_up_bias, ("wide", "narrow"), scatter_dimension=0, tiled=True),
        lax.psum_scatter(grad_down, ("wide", "narrow"), scatter_dimension=0, tiled=True),
        lax.psum_scatter(grad_down_bias, ("wide", "narrow"), scatter_dimension=0, tiled=True),
    )
    attn_back = (
        lax.all_gather(ln1_gain, ("wide", "narrow"), axis=0, tiled=True),
        lax.all_gather(ln1_shift, ("wide", "narrow"), axis=0, tiled=True),
        lax.all_gather(qkv_weight, ("wide", "narrow"), axis=0, tiled=True),
        lax.all_gather(qkv_bias, ("wide", "narrow"), axis=0, tiled=True),
        lax.all_gather(out_weight, ("wide", "narrow"), axis=0, tiled=True),
        lax.all_gather(out_bias, ("wide", "narrow"), axis=0, tiled=True),
    )
    grad_branch = grad_middle.astype(jnp.bfloat16)
    grad_out_weight = weight_grad(attended, grad_branch)
    grad_out_bias = column_sum(grad_branch)
    grad_attended = jnp.einsum(
        "rd,ed->re", grad_branch, attn_back[4], preferred_element_type=jnp.float32
    ).astype(jnp.bfloat16)
    grad_heads = grad_attended.reshape(length, HEADS, HEAD).transpose(1, 0, 2)
    grad_query, grad_key, grad_value = lax.map(
        head_backward, (split[0], split[1], split[2], grad_heads, log_norms)
    )
    grad_qkv = (
        jnp.stack((grad_query, grad_key, grad_value)).transpose(2, 0, 1, 3).reshape(length, 3 * D)
    )
    grad_qkv = grad_qkv.astype(jnp.bfloat16)
    grad_qkv_weight = weight_grad(hidden_one, grad_qkv)
    grad_qkv_bias = column_sum(grad_qkv)
    grad_hidden_one = jnp.einsum(
        "rf,df->rd", grad_qkv, attn_back[2], preferred_element_type=jnp.float32
    )
    grad_gain_one = jnp.sum(grad_hidden_one * normed_one, axis=0)
    grad_shift_one = jnp.sum(grad_hidden_one, axis=0)
    grad_inputs = grad_middle + norm_back(
        grad_hidden_one * attn_back[0].astype(jnp.float32), normed_one, inverse_one
    )
    attn_shares = (
        lax.psum_scatter(grad_gain_one, ("wide", "narrow"), scatter_dimension=0, tiled=True),
        lax.psum_scatter(grad_shift_one, ("wide", "narrow"), scatter_dimension=0, tiled=True),
        lax.psum_scatter(grad_qkv_weight, ("wide", "narrow"), scatter_dimension=0, tiled=True),
        lax.psum_scatter(grad_qkv_bias, ("wide", "narrow"), scatter_dimension=0, tiled=True),
        lax.psum_scatter(grad_out_weight, ("wide", "narrow"), scatter_dimension=0, tiled=True),
        lax.psum_scatter(grad_out_bias, ("wide", "narrow"), scatter_dimension=0, tiled=True),
    )
    return (
        mixed,
        grad_inputs.astype(jnp.bfloat16),
        attn_shares[0],
        attn_shares[1],
        attn_shares[2],
        attn_shares[3],
        attn_shares[4],
        attn_shares[5],
        mlp_shares[0],
        mlp_shares[1],
        mlp_shares[2],
        mlp_shares[3],
        mlp_shares[4],
        mlp_shares[5],
    )


def solution(mesh):
    in_specs = (
        P(("wide", "narrow"), None),
        P(("wide", "narrow"), None),
        P(("wide", "narrow")),
        P(("wide", "narrow")),
        P(("wide", "narrow")),
        P(("wide", "narrow"), None),
        P(("wide", "narrow")),
        P(("wide", "narrow"), None),
        P(("wide", "narrow")),
        P(("wide", "narrow")),
        P(("wide", "narrow")),
        P(("wide", "narrow"), None),
        P(("wide", "narrow")),
        P(("wide", "narrow"), None),
        P(("wide", "narrow")),
    )
    out_specs = (
        P(("wide", "narrow"), None),
        P(("wide", "narrow"), None),
        P(("wide", "narrow")),
        P(("wide", "narrow")),
        P(("wide", "narrow"), None),
        P(("wide", "narrow")),
        P(("wide", "narrow"), None),
        P(("wide", "narrow")),
        P(("wide", "narrow")),
        P(("wide", "narrow")),
        P(("wide", "narrow"), None),
        P(("wide", "narrow")),
        P(("wide", "narrow"), None),
        P(("wide", "narrow")),
    )
    return jax.shard_map(shards, mesh=mesh, in_specs=in_specs, out_specs=out_specs, check_vma=False)
```

profile of v0, /device:TPU:0, one launch (start us, length us, event | category | flops | bytes accessed | tf_op | source)
XLA Modules:
  0.0 939.1 jit_solution(5906381281078058114)
XLA Ops:
  16.8 42.7 %all-reduce.17 = (bf16[2304]{0:T(1024)(128)(2,1)S(1)}, bf16[768]{0:T(1024)(128)(2,1)S(1)}, bf16[768]{0:T(1024)(128)(2,1)S(1)}, bf16[768]{0:T(1024)(128)(2,1)S(1)...) all-reduce(bf16[2304]{0:T(1024)(128)(2,1)S(1)} %dynamic-update-slic, ...), channel_id=1, replica_groups=mesh['wide'=16,'narrow'=2] {'wide','narrow'}, use_global_device_ids=true, to_apply=%add.2 | all-reduce | flops 9984 | bytes 39936
  64.5 9.4 %all-gather.5.cloned.1.call-done = bf16[768,2304]{1,0:T(8,128)(2,1)} async-done(((bf16[24,2304]{1,0:T(8,128)(2,1)}), bf16[768,2304]{1,0:T(8,128)(2,1)}) %all-gather.5.cloned.1.call-update) | async-done | bytes 3538960 | tf_op jit(solution)/shard_map/all_gather | solution.py:98
  73.9 7.9 add_convert_fusion
  81.8 6.6 copy.58
  105.7 121.3 %while.26 = (s32[]{:T(128)}, bf16[12,1024,64]{1,2,0:T(8,128)(2,1)}, f32[12,1024]{1,0:T(8,128)S(1)}, bf16[12,1024,64]{2,1,0:T(8,128)(2,1)S(1)}, bf16[12,1024,64]{...) while((s32[]{:T(128)}, bf16[12,1024,64]{1,2,0:T(8,128)(2,1)}, ...), condition=%wide.region_5.6_spmd, body=%wide.region_2.5_spmd.sunk | while | flops 293600256 | bytes 30451828 | solution.py:112
  191.7 4.9 fusion.122
  233.0 10.6 %fusion.84 = f32[1024,3072]{1,0:T(8,128)} fusion(bf16[768,3072]{1,0:T(8,128)(2,1)} %all-gather.9.cloned.1.call-done, f32[1024,768]{0,1:T(8,128)S(1)} %get-tuple-element.238, f32[768]{0:T(1024)S(1)} %convert_element_type.111, f32[768]{0:T(1024)S(1)} %convert_element_type.110, f32[1024]{0:T(1024)S(1)} %add_rsqrt_fusion, f32[1024]{0:T(1024)S(1)} %broadcast_multiply_fusion.4), kind=kOutput, calls=%fused_computation.132 | convolution fusion | flops 4835770368 | bytes 20461568 | tf_op jit(solution)/shard_map/dot_general | solution.py:130
  243.7 16.9 %all-gather.11.cloned.1.call-done = bf16[3072,768]{1,0:T(8,128)(2,1)} async-done(((bf16[96,768]{1,0:T(8,128)(2,1)}), bf16[3072,768]{1,0:T(8,128)(2,1)}) %all-gather.11.cloned.1.call-update) | async-done | bytes 4718608 | tf_op jit(solution)/shard_map/all_gather | solution.py:124
  260.6 17.0 %convert_reduce_fusion = (f32[3072]{0:T(1024)S(1)}, bf16[1024,3072]{1,0:T(8,128)(2,1)S(1)}) fusion(f32[1024,3072]{1,0:T(8,128)} %fusion.84, f32[3072]{0:T(1024)S(1)} %convert_element_type.113, bf16[3072,768]{1,0:T(8,128)(2,1)} %all-gather.11.cloned.1.call-done, bf16[1024,768]{0,1:T(8,128)(2,1)} %copy.63, pred[1024]{0:T(1024)(128)(4,1)S(1)} %iota_compare_fusion.2), kind=kOutput, calls=%fused_computation.73 | convolution fusion | flops 4904973312 | bytes 25191424 | tf_op jit(solution)/shard_map/rd,fd->rf/dot_general | solution.py:154
  277.6 6.7 fusion.87
  310.5 207.5 %while.27 = (s32[]{:T(128)}, bf16[12,1024,64]{1,2,0:T(8,128)(2,1)}, bf16[12,1024,64]{1,2,0:T(8,128)(2,1)}, bf16[12,1024,64]{1,2,0:T(8,128)(2,1)}, bf16[12,1024,6...) while((s32[]{:T(128)}, bf16[12,1024,64]{1,2,0:T(8,128)(2,1)}, ...), condition=%wide.region_12.13_spmd, body=%wide.region_10.12_spmd.sunk | while | flops 707918848 | bytes 34112616 | solution.py:189
  315.3 4.8 select_convert_fusion.2
  332.6 4.8 select_convert_fusion.2
  349.9 4.8 select_convert_fusion.2
  367.2 4.8 select_convert_fusion.2
  384.4 4.8 select_convert_fusion.2
  401.7 4.8 select_convert_fusion.2
  419.0 4.8 select_convert_fusion.2
  436.2 4.8 select_convert_fusion.2
  453.5 4.8 select_convert_fusion.2
  470.8 4.8 select_convert_fusion.2
  488.1 4.8 select_convert_fusion.2
  523.1 6.4 fusion.80
  529.6 10.5 %fusion.83 = f32[768,3072]{1,0:T(8,128)} fusion(bf16[1024,3072]{1,0:T(8,128)(2,1)} %copy-done.20, f32[1024,768]{0,1:T(8,128)S(1)} %get-tuple-element.238, f32[768]{0:T(1024)S(1)} %convert_element_type.111, f32[768]{0:T(1024)S(1)} %convert_element_type.110, f32[1024]{0:T(1024)S(1)} %add_rsqrt_fusion, f32[1024]{0:T(1024)S(1)} %broadcast_multiply_fusion.4), kind=kOutput, calls=%fused_computation.131 | convolution fusion | flops 4835770368 | bytes 18888704 | tf_op jit(solution)/shard_map/rd,rf->df/dot_general | solution.py:74
  540.2 14.8 %fusion.72 = f32[3072,768]{1,0:T(8,128)} fusion(bf16[1024,768]{0,1:T(8,128)(2,1)} %copy.63, pred[1024]{0:T(1024)(128)(4,1)S(1)} %iota_compare_fusion.2, f32[1024,3072]{1,0:T(8,128)} %fusion.84, f32[3072]{0:T(1024)S(1)} %convert_element_type.113), kind=kOutput, calls=%fused_computation.113 | convolution fusion | flops 4864081920 | bytes 23606272 | tf_op jit(solution)/shard_map/rd,rf->df/dot_general | solution.py:74
  555.6 9.2 fusion.86
  572.0 42.7 %all-reduce.16 = (f32[768]{0:T(1024)S(1)}, f32[768]{0:T(1024)S(1)}, f32[2304]{0:T(1024)S(1)}, f32[768]{0:T(1024)S(1)}, f32[768]{0:T(1024)S(1)}, /*index=5*/f32[7...) all-reduce(f32[768]{0:T(1024)S(1)} %get-tuple-element.175, ...), channel_id=2, replica_groups=mesh['wide'=16,'narrow'=2] {'wide','narrow'}, use_global_device_ids=true, to_apply=%region_16.17.clone | all-reduce | flops 9984 | bytes 79872
  618.2 5.5 fusion.68
  626.3 11.9 %add_convert_fusion.1 = bf16[1024,768]{0,1:T(8,128)(2,1)} fusion(f32[1024,768]{0,1:T(8,128)S(1)} %get-tuple-element.238, bf16[3072,768]{1,0:T(8,128)(2,1)} %all-gather.11.cloned.1.call-done, f32[768]{0:T(1024)S(1)} %convert_element_type.115, f32[1024,3072]{1,0:T(8,128)} %fusion.84, f32[3072]{0:T(1024)S(1)} %convert_element_type.113), kind=kOutput, calls=%fused_computation.102 | convolution fusion | flops 4865654784 | bytes 22035456 | tf_op jit(solution)/shard_map/dot_general | solution.py:137
  641.9 6.4 reduce-scatter.5.cloned.1.call-done
  648.3 141.5 %reduce-scatter.9.cloned.1.call-done = f32[24,3072]{1,0:T(8,128)} async-done(((f32[768,3072]{1,0:T(8,128)}), f32[24,3072]{1,0:T(8,128)}) %reduce-scatter.9.cloned.1.call-update) | async-done | bytes 294928 | tf_op jit(solution)/shard_map/reduce_scatter | solution.py:169
  789.8 142.1 %reduce-scatter.11.cloned.1.call-done = f32[96,768]{1,0:T(8,128)} async-done(((f32[3072,768]{1,0:T(8,128)}), f32[96,768]{1,0:T(8,128)}) %reduce-scatter.11.cloned.1.call-update) | async-done | bytes 294928 | tf_op jit(solution)/shard_map/reduce_scatter | solution.py:171
  (282 shorter events, 355.6 us)
Async XLA Ops:
  7.2 66.7 %all-gather.5.cloned.1.call-start = ((), (), s32[]{:S(2)}) async-start(), calls=%async_computation.4 | async-start | bytes 3649536 | tf_op jit(solution)/shard_map/all_gather | solution.py:98
  7.9 219.1 %all-gather.7.cloned.1.call-start = ((), (), s32[]{:S(2)}) async-start(), calls=%async_computation.5 | async-start | bytes 1216512 | tf_op jit(solution)/shard_map/all_gather | solution.py:100
  8.7 224.4 %all-gather.9.cloned.1.call-start = ((), (), s32[]{:S(2)}) async-start(), calls=%async_computation.6 | async-start | bytes 4866048 | tf_op jit(solution)/shard_map/all_gather | solution.py:122
  9.4 251.2 %all-gather.11.cloned.1.call-start = ((), (), s32[]{:S(2)}) async-start(), calls=%async_computation.7 | async-start | bytes 4866048 | tf_op jit(solution)/shard_map/all_gather | solution.py:124
  10.0 631.9 %reduce-scatter.7.cloned.1.call-start = ((), (), s32[]{:S(2)}) async-start(), calls=%async_computation.9 | async-start | bytes 2433024 | tf_op jit(solution)/shard_map/reduce_scatter | solution.py:211
  59.5 14.4 %copy-start.13 = (f32[768]{0:T(1024)}, f32[768]{0:T(1024)S(1)}, u32[]{:S(2)}) copy-start(f32[768]{0:T(1024)S(1)} %convert_element_type.101) | copy-start | bytes 9220
  59.5 14.4 %copy-start.17 = (f32[768]{0:T(1024)}, f32[768]{0:T(1024)S(1)}, u32[]{:S(2)}) copy-start(f32[768]{0:T(1024)S(1)} %convert_element_type.102) | copy-start | bytes 9220
  59.5 2.7 copy-start.9
  61.3 12.6 %copy-start.1 = (bf16[1024,768]{0,1:T(8,128)(2,1)}, bf16[1024,768]{0,1:T(8,128)(2,1)S(1)}, u32[]{:S(2)}) copy-start(bf16[1024,768]{0,1:T(8,128)(2,1)S(1)} %copy.57) | copy-start | bytes 4718596
  61.6 20.1 %copy-start.11 = (f32[1024]{0:T(1024)}, f32[1024]{0:T(1024)S(1)}, u32[]{:S(2)}) copy-start(f32[1024]{0:T(1024)S(1)} %broadcast_multiply_fusion.5) | copy-start | bytes 12292
  62.1 19.7 %copy-start.15 = (f32[1024]{0:T(1024)}, f32[1024]{0:T(1024)S(1)}, u32[]{:S(2)}) copy-start(f32[1024]{0:T(1024)S(1)} %add_rsqrt_fusion.1) | copy-start | bytes 12292
  117.9 1.9 copy-start
  128.0 1.9 copy-start
  158.2 1.9 copy-start
  168.3 1.9 copy-start
  178.4 1.9 copy-start
  188.5 1.9 copy-start
  198.7 1.9 copy-start
  260.6 17.0 %copy-start.7 = (bf16[768,3072]{1,0:T(8,128)(2,1)S(1)}, bf16[768,3072]{1,0:T(8,128)(2,1)}, u32[]{:S(2)}) copy-start(bf16[768,3072]{1,0:T(8,128)(2,1)} %all-gather.9.cloned.1.call-done) | copy-start | bytes 14155780
  277.6 6.8 copy-start.20
  287.9 3.0 copy-start.3
  287.9 3.3 copy-start.6
  291.2 3.5 copy-start.10
  306.4 341.9 %reduce-scatter.5.cloned.1.call-start = ((), (), s32[]{:S(2)}) async-start(), calls=%async_computation.8 | async-start | bytes 7299072 | tf_op jit(solution)/shard_map/reduce_scatter | solution.py:209
  518.0 5.1 copy-start.2
  518.0 5.1 copy-start.12
  518.0 5.1 copy-start.14
  518.0 5.1 copy-start.16
  518.0 5.1 copy-start.18
  520.9 2.2 copy-start.8
  529.5 260.3 %reduce-scatter.9.cloned.1.call-start = ((), (), s32[]{:S(2)}) async-start(), calls=%async_computation.10 | async-start | bytes 9732096 | tf_op jit(solution)/shard_map/reduce_scatter | solution.py:169
  540.1 391.7 %reduce-scatter.11.cloned.1.call-start = ((), (), s32[]{:S(2)}) async-start(), calls=%async_computation.11 | async-start | bytes 9732096 | tf_op jit(solution)/shard_map/reduce_scatter | solution.py:171
  (8 other events, 13.7 us)
Sparse Core Ops, SparseCore 0:
  10.9 62.9 all-gather.4
  76.8 52.9 all-gather.6
  132.7 62.6 all-gather.8
  198.1 62.3 all-gather.10
  306.5 97.8 reduce-scatter.6
  529.7 118.6 reduce-scatter.4
  654.8 134.9 reduce-scatter.8
  797.3 134.5 reduce-scatter.10
where the time goes:
time: 951 us; the launch traced here: 939 us
  matrix products  338 us (36%)
  waiting for transfers between devices  319 us (34%)
  local copies, waits for them, and re-layouts  90.3 us (9%)
  other arithmetic  89.9 us (9%)
  blocking collectives  85.4 us (9%)
  between operations  15.6 us (2%)
    reduce_scatter x1, waiting for transfers between devices, shards(): lax.psum_scatter(grad_down, ('wide', 'narrow'), scatter_dimension=0, tile...  142 us
    reduce_scatter x1, waiting for transfers between devices, shards(): lax.psum_scatter(grad_up, ('wide', 'narrow'), scatter_dimension=0, tiled=...  141 us
    unnamed x2, blocking collectives  85.4 us
    convert_element_type x12, other arithmetic, head_backward(): grad_scores = jnp.where(causal, grad_scores, 0.0).astype(jnp.bfloat16)  58.2 us
    dot_general x12, matrix products, head_forward(): result = jnp.dot(weights, value_rows, preferred_element_type=jnp.float32)  56.7 us
    dot_general x24, matrix products, head_scores(): jnp.einsum('qd,kd->qk', query, key_rows, preferred_element_type=jnp.float32)  46.7 us
    dot_general x12, matrix products, head_backward(): jnp.einsum('qk,qd->kd', weights, grad_out, preferred_element_type=jnp.flo...  39.1 us
    dot_general x4, matrix products, weight_grad(): jnp.einsum('rd,rf->df', left, right, preferred_element_type=jnp.float32)  34.5 us
  transfers between devices with their start and end apart: 8, of which 5 were waited for; matrix products, arithmetic and copies ran while one was open for 47% of the time, Pallas kernels for 0%

commit v1 on v0

v1 whole, which is shorter than its diff:
```python
import functools

import jax
import jax.numpy as jnp
from jax import lax
from jax.experimental import pallas as pl
from jax.experimental.pallas import tpu as pltpu
from jax.sharding import PartitionSpec as P

D = 768
FF = 3072
HEADS = 12
HEAD = 64
BLK = 256
AXES = ("wide", "narrow")
MESH = pl.DeviceIdType.MESH
VMEM = pltpu.VMEM
F32 = jnp.float32
BF16 = jnp.bfloat16


def nn(left, right):
    return lax.dot_general(left, right, (((1,), (0,)), ((), ())), preferred_element_type=F32)


def nt(left, right):
    return lax.dot_general(left, right, (((1,), (1,)), ((), ())), preferred_element_type=F32)


def norm_parts(values):
    average = jnp.mean(values, axis=-1, keepdims=True)
    centered = values - average
    inverse = lax.rsqrt(jnp.mean(centered * centered, axis=-1, keepdims=True) + 1e-05)
    return centered * inverse, inverse


def norm_back(grad_normed, normed, inverse):
    first_mean = jnp.mean(grad_normed, axis=-1, keepdims=True)
    second_mean = jnp.mean(grad_normed * normed, axis=-1, keepdims=True)
    return inverse * (grad_normed - first_mean - normed * second_mean)


def lane_half(values, half):
    lanes = lax.broadcasted_iota(jnp.int32, values.shape, 1)
    keep = (lanes < HEAD) if half == 0 else (lanes >= HEAD)
    return jnp.where(keep, values, jnp.zeros_like(values))


def diagonal_keep():
    keys = lax.broadcasted_iota(jnp.int32, (BLK, BLK), 0)
    queries = lax.broadcasted_iota(jnp.int32, (BLK, BLK), 1)
    return keys <= queries


def column(pair, part):
    return pl.ds(pl.multiple_of(part * D + pair * 128, 128), 128)


def qkv_rows(block, x_ref, vec24_ref, vec72_ref, wqkv_ref, qkv_ref):
    rows = pl.ds(pl.multiple_of(block * BLK, BLK), BLK)
    normed, _ = norm_parts(x_ref[rows, :].astype(F32))
    hidden = (normed * vec24_ref[0:1, :] + vec24_ref[1:2, :]).astype(BF16)
    for part in range(3):
        cols = slice(part * D, (part + 1) * D)
        qkv_ref[rows, cols] = (nn(hidden, wqkv_ref[:, cols]) + vec72_ref[6:7, cols]).astype(BF16)


def attention_pair(pair, qkv_ref, o_ref, lse_ref, vt):
    length = qkv_ref.shape[0]
    vt[...] = qkv_ref[:, column(pair, 2)].T
    keep = diagonal_keep()
    for j in range(length // BLK):
        span = (j + 1) * BLK
        rows = slice(j * BLK, span)
        query = qkv_ref[rows, column(pair, 0)] * jnp.asarray(0.125, BF16)
        keys = qkv_ref[0:span, column(pair, 1)]
        outs = []
        for half in range(2):
            s = nt(keys, lane_half(query, half))
            w = s * s + 1.0
            m = w * lax.rsqrt(w)
            tail = jnp.where(keep, m[j * BLK :], -1e30)
            m = tail if j == 0 else jnp.concatenate([m[: j * BLK], tail], axis=0)
            top = jnp.max(m, axis=0, keepdims=True)
            e = jnp.exp(m - top)
            total = jnp.sum(e, axis=0, keepdims=True)
            a = (jnp.tanh(s) * e).astype(BF16)
            outs.append(nn(vt[half * HEAD : (half + 1) * HEAD, 0:span], a) / total)
            lse_ref[pair, half : half + 1, rows] = top + jnp.log(total)
        o_ref[rows, column(pair, 0)] = jnp.concatenate(outs, axis=0).T.astype(BF16)


def attention_back_pair(pair, qkv_ref, o_ref, do_ref, lse_ref, dqkv_ref, kt, dk, dv):
    length = qkv_ref.shape[0]
    kt[...] = qkv_ref[:, column(pair, 1)].T
    keep = diagonal_keep()
    lanes = lax.broadcasted_iota(jnp.int32, (8, 128), 1)
    sublanes = lax.broadcasted_iota(jnp.int32, (8, 128), 0)
    pick = (lanes // HEAD == sublanes).astype(F32)
    steps = length // BLK
    for j in reversed(range(steps)):
        span = (j + 1) * BLK
        rows = slice(j * BLK, span)
        query = qkv_ref[rows, column(pair, 0)] * jnp.asarray(0.125, BF16)
        grad = do_ref[rows, column(pair, 0)]
        product = grad.astype(F32) * o_ref[rows, column(pair, 0)].astype(F32)
        inner = lax.dot_general(
            pick, product, (((1,), (1,)), ((), ())),
            precision=lax.Precision.HIGHEST, preferred_element_type=F32,
        )
        keys = qkv_ref[0:span, column(pair, 1)]
        values = qkv_ref[0:span, column(pair, 2)]
        dqs = []
        dks = None
        dvs = None
        for half in range(2):
            query_half = lane_half(query, half)
            grad_half = lane_half(grad, half)
            s = nt(keys, query_half)
            da = nt(values, grad_half)
            w = s * s + 1.0
            r = lax.rsqrt(w)
            p = jnp.exp(w * r - lse_ref[pair, half : half + 1, rows])
            tail = jnp.where(keep, p[j * BLK :], 0.0)
            p = tail if j == 0 else jnp.concatenate([p[: j * BLK], tail], axis=0)
            t = jnp.tanh(s)
            a = (t * p).astype(BF16)
            ds = p * (da * (1.0 - t * t) + (da * t - inner[half : half + 1, :]) * (s * r))
            ds = ds.astype(BF16)
            dqs.append(nn(kt[half * HEAD : (half + 1) * HEAD, 0:span], ds))
            this_dk = nn(ds, query_half)
            this_dv = nn(a, grad_half)
            dks = this_dk if half == 0 else dks + this_dk
            dvs = this_dv if half == 0 else dvs + this_dv
        dqkv_ref[rows, column(pair, 0)] = (jnp.concatenate(dqs, axis=0).T * 0.125).astype(BF16)
        if j == steps - 1:
            dk[...] = dks
            dv[...] = dvs
        else:
            dk[0:span, :] += dks
            dv[0:span, :] += dvs
    dqkv_ref[:, column(pair, 1)] = dk[...].astype(BF16)
    dqkv_ref[:, column(pair, 2)] = dv[...].astype(BF16)


def forward_kernel(x_ref, vec24_ref, vec72_ref, wqkv_ref, qkv_ref, o_ref, lse_ref, vt):
    lax.fori_loop(
        0,
        x_ref.shape[0] // BLK,
        lambda b, c: (qkv_rows(b, x_ref, vec24_ref, vec72_ref, wqkv_ref, qkv_ref), c)[1],
        0,
    )
    lax.fori_loop(
        0, HEADS // 2, lambda p, c: (attention_pair(p, qkv_ref, o_ref, lse_ref, vt), c)[1], 0
    )


def forward_call(x, vec24, vec72, wqkv):
    length = x.shape[0]
    return pl.pallas_call(
        forward_kernel,
        out_shape=(
            jax.ShapeDtypeStruct((length, 3 * D), BF16),
            jax.ShapeDtypeStruct((length, D), BF16),
            jax.ShapeDtypeStruct((HEADS // 2, 8, length), F32),
        ),
        in_specs=[pl.BlockSpec(memory_space=VMEM)] * 4,
        out_specs=(pl.BlockSpec(memory_space=VMEM),) * 3,
        scratch_shapes=[VMEM((128, length), BF16)],
        compiler_params=pltpu.CompilerParams(vmem_limit_bytes=56 * 2**20),
    )(x, vec24, vec72, wqkv)


def store_blocks(out_ref, first, count, value):
    depth = out_ref.shape[1]
    out_ref[pl.ds(first, count)] = value.reshape(count, depth, value.shape[1]).astype(BF16)


def middle_kernel(
    len_ref, x_ref, o_ref, cot_ref, vec24_ref, vec96_ref, wout_ref, wup_ref, wdown_ref,
    mixed_ref, do_ref, dy1_ref, gout_ref, gup_ref, gdown_ref, small24_ref, small96_ref,
    f_t, du, h2_t, dy, dz, o_t,
):
    step = pl.program_id(0)
    steps = pl.num_programs(0)
    rows_at = pl.multiple_of(step * BLK, BLK)
    here = pl.ds(rows_at, BLK)
    chunk = 768

    @pl.when(step == 0)
    def _():
        small24_ref[...] = jnp.zeros_like(small24_ref)
        small96_ref[...] = jnp.zeros_like(small96_ref)

    attended = o_ref[...]
    y1 = x_ref[...].astype(F32) + nn(attended, wout_ref[...]) + vec24_ref[2:3, :]
    normed, inverse = norm_parts(y1)
    h2 = (normed * vec24_ref[3:4, :] + vec24_ref[4:5, :]).astype(BF16)
    rows = lax.broadcasted_iota(jnp.int32, (BLK, D), 0) + rows_at
    upstream = jnp.where(rows < len_ref[0], cot_ref[...].astype(F32), 0.0)
    upstream16 = upstream.astype(BF16)
    y = y1 + vec24_ref[5:6, :]
    dh2 = None
    for c in range(FF // chunk):
        cols = slice(c * chunk, (c + 1) * chunk)
        u = nn(h2, wup_ref[:, cols]) + vec96_ref[7:8, cols]
        square = u * u
        t = jnp.tanh(u * (0.7978845608028654 + 0.035677408136300125 * square))
        half = 0.5 * (1.0 + t)
        f = (u * half).astype(BF16)
        slope = half + (0.5 * u) * (1.0 - t * t) * (
            0.7978845608028654 + 0.10703222440890037 * square
        )
        y = y + nn(f, wdown_ref[cols, :])
        df = nt(upstream16, wdown_ref[cols, :])
        d16 = (df * slope).astype(BF16)
        du[here, cols] = d16
        f_t[cols, here] = f.T
        small96_ref[7:8, cols] += jnp.sum(d16.astype(F32), axis=0, keepdims=True)
        part = nt(d16, wup_ref[:, cols])
        dh2 = part if c == 0 else dh2 + part
    mixed_ref[...] = y.astype(BF16)
    e = dh2 * vec24_ref[3:4, :]
    dy1 = upstream + norm_back(e, normed, inverse)
    dz16 = dy1.astype(BF16)
    dy1_ref[...] = dy1
    do_ref[...] = nt(dz16, wout_ref[...]).astype(BF16)
    small24_ref[2:3, :] += jnp.sum(dz16.astype(F32), axis=0, keepdims=True)
    small24_ref[3:4, :] += jnp.sum(dh2 * normed, axis=0, keepdims=True)
    small24_ref[4:5, :] += jnp.sum(dh2, axis=0, keepdims=True)
    small24_ref[5:6, :] += jnp.sum(upstream, axis=0, keepdims=True)
    h2_t[:, here] = h2.T
    o_t[:, here] = attended.T
    dy[here, :] = upstream16
    dz[here, :] = dz16

    @pl.when(step == steps - 1)
    def _():
        shards = gout_ref.shape[0]
        many = shards // 4
        deep = gdown_ref.shape[1] * many // 4

        def one(i, carry):
            first = pl.multiple_of(i * many, many)
            left = pl.ds(pl.multiple_of(i * (D // 4), D // 4), D // 4)
            store_blocks(gout_ref, first, many, nn(o_t[left, :], dz[...]))
            for c in range(FF // chunk):
                cols = slice(c * chunk, (c + 1) * chunk)
                value = nn(h2_t[left, :], du[:, cols]).reshape(many, D // shards, chunk)
                gup_ref[pl.ds(first, many), :, cols] = value.astype(BF16)
            return carry

        lax.fori_loop(0, 4, one, 0)

        def two(i, carry):
            left = pl.ds(pl.multiple_of(i * deep, deep), deep)
            store_blocks(gdown_ref, i * (many // 4), many // 4, nn(f_t[left, :], dy[...]))
            return carry

        lax.fori_loop(0, 16, two, 0)


def middle_call(lengths, x, attended, cotangent, vec24, vec96, wout, wup, wdown, shards):
    length = x.shape[0]

    def rows(width):
        return pl.BlockSpec((BLK, width), lambda i: (i, 0))

    def whole(shape):
        return pl.BlockSpec(
            shape, lambda i: (0,) * len(shape), pipeline_mode=pl.Buffered(1)
        )

    outs = (
        ((length, D), BF16, rows(D)),
        ((length, D), BF16, rows(D)),
        ((length, D), F32, rows(D)),
        ((shards, D // shards, D), BF16, None),
        ((shards, D // shards, FF), BF16, None),
        ((shards, FF // shards, D), BF16, None),
        ((16, D), F32, None),
        ((16, FF), F32, None),
    )
    return pl.pallas_call(
        middle_kernel,
        grid=(length // BLK,),
        out_shape=tuple(jax.ShapeDtypeStruct(s, t) for s, t, _ in outs),
        in_specs=[
            pl.BlockSpec(memory_space=pltpu.SMEM),
            rows(D), rows(D), rows(D),
            whole(vec24.shape), whole(vec96.shape),
            whole(wout.shape), whole(wup.shape), whole(wdown.shape),
        ],
        out_specs=tuple(whole(s) if b is None else b for s, _, b in outs),
        scratch_shapes=[
            VMEM((FF, length), BF16),
            VMEM((length, FF), BF16),
            VMEM((D, length), BF16),
            VMEM((length, D), BF16),
            VMEM((length, D), BF16),
            VMEM((D, length), BF16),
        ],
        compiler_params=pltpu.CompilerParams(
            dimension_semantics=("arbitrary",), vmem_limit_bytes=60 * 2**20
        ),
    )(lengths, x, attended, cotangent, vec24, vec96, wout, wup, wdown)


def tail_rows(block, x_ref, dy1_ref, vec24_ref, wqkv_ref, dqkv_ref, h1_t, gx_ref, s24_ref, s72_ref):
    here = pl.ds(pl.multiple_of(block * BLK, BLK), BLK)
    normed, inverse = norm_parts(x_ref[here, :].astype(F32))
    hidden = (normed * vec24_ref[0:1, :] + vec24_ref[1:2, :]).astype(BF16)
    h1_t[:, here] = hidden.T
    grad = dqkv_ref[here, :]
    dh1 = nt(grad, wqkv_ref[...])
    e = dh1 * vec24_ref[0:1, :]
    gx_ref[here, :] = (dy1_ref[here, :] + norm_back(e, normed, inverse)).astype(BF16)
    s24_ref[0:1, :] += jnp.sum(dh1 * normed, axis=0, keepdims=True)
    s24_ref[1:2, :] += jnp.sum(dh1, axis=0, keepdims=True)
    s72_ref[6:7, :] += jnp.sum(grad.astype(F32), axis=0, keepdims=True)


def backward_kernel(
    x_ref, dy1_ref, vec24_ref, wqkv_ref, qkv_ref, o_ref, do_ref, lse_ref,
    gx_ref, gqkv_ref, s24_ref, s72_ref,
    dqkv, h1_t, kt, dk, dv,
):
    s24_ref[...] = jnp.zeros_like(s24_ref)
    s72_ref[...] = jnp.zeros_like(s72_ref)
    lax.fori_loop(
        0,
        HEADS // 2,
        lambda p, c: (
            attention_back_pair(p, qkv_ref, o_ref, do_ref, lse_ref, dqkv, kt, dk, dv),
            c,
        )[1],
        0,
    )
    lax.fori_loop(
        0,
        x_ref.shape[0] // BLK,
        lambda b, c: (
            tail_rows(
                b, x_ref, dy1_ref, vec24_ref, wqkv_ref, dqkv, h1_t, gx_ref, s24_ref, s72_ref
            ),
            c,
        )[1],
        0,
    )
    shards = gqkv_ref.shape[0]
    many = shards // 4

    def one(i, carry):
        left = pl.ds(pl.multiple_of(i * (D // 4), D // 4), D // 4)
        for part in range(3):
            cols = slice(part * D, (part + 1) * D)
            value = nn(h1_t[left, :], dqkv[:, cols]).reshape(many, D // shards, D)
            gqkv_ref[pl.ds(i * many, many), :, cols] = value.astype(BF16)
        return carry

    lax.fori_loop(0, 4, one, 0)


def backward_call(x, dy1, vec24, wqkv, qkv, attended, grad_attended, lse, shards):
    length = x.shape[0]
    return pl.pallas_call(
        backward_kernel,
        out_shape=(
            jax.ShapeDtypeStruct((length, D), BF16),
            jax.ShapeDtypeStruct((shards, D // shards, 3 * D), BF16),
            jax.ShapeDtypeStruct((16, D), F32),
            jax.ShapeDtypeStruct((16, 3 * D), F32),
        ),
        in_specs=[pl.BlockSpec(memory_space=VMEM)] * 8,
        out_specs=(pl.BlockSpec(memory_space=VMEM),) * 4,
        scratch_shapes=[
            VMEM((length, 3 * D), BF16),
            VMEM((D, length), BF16),
            VMEM((128, length), BF16),
            VMEM((length, 128), F32),
            VMEM((length, 128), F32),
        ],
        compiler_params=pltpu.CompilerParams(vmem_limit_bytes=60 * 2**20),
    )(x, dy1, vec24, wqkv, qkv, attended, grad_attended, lse)


def place():
    wide = lax.axis_index("wide")
    return wide // 4, (wide // 2) % 2, wide % 2, lax.axis_index("narrow")


def device(z, x, c, y):
    return ((z * 2 + x) * 2 + c, y)


def greet():
    z, x, c, y = place()
    barrier = pltpu.get_barrier_semaphore()
    peers = [device(lax.rem(z + d, 4), x, c, y) for d in (1, 2, 3)]
    peers += [device(z, 1 - x, c, y), device(z, x, c, 1 - y), device(z, x, 1 - c, y)]
    for peer in peers:
        pl.semaphore_signal(barrier, inc=1, device_id=peer, device_id_type=MESH)
    pl.semaphore_wait(barrier, len(peers))


def remote(src, dst, sems, slot, peer):
    return pltpu.make_async_remote_copy(
        src_ref=src, dst_ref=dst, send_sem=sems[0].at[slot], recv_sem=sems[1].at[slot],
        device_id=peer, device_id_type=MESH,
    )


class Gather:
    slots = 12

    def __init__(self, own, full, sems, local_sem):
        self.own, self.full, self.sems, self.local = own, full, sems, local_sem
        width = full.shape[-1]
        cut = width // 256 * 128
        self.first = pl.ds(0, cut or width)
        self.second = pl.ds(cut, width - cut) if cut else None
        z, x, c, y = place()
        self.peer_x = device(z, 1 - x, c, y)
        self.peer_y = device(z, x, c, 1 - y)
        self.peer_c = device(z, x, 1 - c, y)
        self.at = (z, x, c, y)
        self.copies = []

    def send(self, slot, peer, *index):
        view = self.full.at[index]
        copy = remote(view, view, self.sems, slot, peer)
        copy.start()
        self.copies.append(copy)
        return copy

    def stage0(self):
        z, x, c, y = self.at
        target = self.full.at[z, x, c, y]
        self.keep = pltpu.make_async_copy(self.own, target, self.local)
        self.keep.start()
        self.pending = []
        for d in (2, 1, 3):
            copy = remote(self.own, target, self.sems, d - 1, device(lax.rem(z + d, 4), x, c, y))
            copy.start()
            self.copies.append(copy)
            self.pending.append(copy)

    def land(self):
        for copy in self.pending:
            copy.wait_recv()
        self.pending = []

    def stage1(self):
        z, x, c, y = self.at
        self.keep.wait()
        self.land()
        every = slice(None)
        self.pending = [self.send(3, self.peer_x, every, x, c, y, every, self.first)]
        if self.second is not None:
            self.pending.append(self.send(4, self.peer_y, every, x, c, y, every, self.second))
        self.core = [self.send(5, self.peer_c, every, x, c, y)]

    def stage2(self):
        z, x, c, y = self.at
        self.land()
        every = slice(None)
        self.pending = [self.send(6, self.peer_y, every, every, c, y, every, self.first)]
        self.core.append(self.send(7, self.peer_c, every, 1 - x, c, y, every, self.first))
        if self.second is not None:
            self.pending.append(self.send(8, self.peer_x, every, x, c, every, every, self.second))
            self.core.append(self.send(9, self.peer_c, every, x, c, 1 - y, every, self.second))

    def stage3(self):
        z, x, c, y = self.at
        self.land()
        every = slice(None)
        self.core.append(self.send(10, self.peer_c, every, every, c, 1 - y, every, self.first))
        if self.second is not None:
            self.core.append(self.send(11, self.peer_c, every, 1 - x, c, every, every, self.second))

    def stage4(self):
        for copy in self.core:
            copy.wait_recv()

    def finish(self):
        for copy in self.copies:
            copy.wait_send()


def spread(blocks, each):
    width = 32 * each
    lane = lax.broadcasted_iota(jnp.int32, (128, width), 0)
    col = lax.broadcasted_iota(jnp.int32, (128, width), 1)
    value = nn(blocks, (lax.rem(col, each) == lane).astype(BF16)).reshape(32, 16, width)
    shard = lax.broadcasted_iota(jnp.int32, (32, 16, width), 0)
    col = lax.broadcasted_iota(jnp.int32, (32, 16, width), 2)
    inside = (col >= shard * each) & (col < shard * each + each)
    return jnp.sum(jnp.where(inside, value, 0.0), axis=0)


def gather_kernel(small, wqkv, wout, wup, wdown, *refs):
    full = refs[1:5]
    vec_refs = refs[5:8]
    small_full = refs[0]
    send, recv, local = refs[8:11]
    greet()
    parts = []
    for i, (own, out) in enumerate(zip((small, wqkv, wout, wup, wdown), (small_full, *full))):
        parts.append(Gather(own, out, (send.at[i], recv.at[i]), local.at[i]))
    for stage in ("stage0", "stage1", "stage2", "stage3", "stage4", "finish"):
        for part in parts:
            getattr(part, stage)()
    blocks = small_full[...].reshape(32 * 16, 128)
    for ref, each in zip(vec_refs, (24, 72, 96)):
        ref[...] = spread(blocks, each)


def gather_call(small, wqkv, wout, wup, wdown):
    own = (small, wqkv, wout, wup, wdown)
    full = tuple(jax.ShapeDtypeStruct((4, 2, 2, 2, *a.shape), BF16) for a in own)
    anywhere = pl.BlockSpec(memory_space=pl.ANY)
    inside = pl.BlockSpec(memory_space=VMEM)
    return pl.pallas_call(
        gather_kernel,
        out_shape=(
            *full,
            jax.ShapeDtypeStruct((16, D), F32),
            jax.ShapeDtypeStruct((16, 3 * D), F32),
            jax.ShapeDtypeStruct((16, FF), F32),
        ),
        in_specs=[inside] + [anywhere] * 4,
        out_specs=(inside, *[anywhere] * 4, *[inside] * 3),
        scratch_shapes=[
            pltpu.SemaphoreType.DMA((5, Gather.slots)),
            pltpu.SemaphoreType.DMA((5, Gather.slots)),
            pltpu.SemaphoreType.DMA((5,)),
        ],
        compiler_params=pltpu.CompilerParams(
            collective_id=1, has_side_effects=True, vmem_limit_bytes=40 * 2**20
        ),
    )(*own)


class Scatter:
    slots = 11

    def __init__(self, grads, out, buffers, sems):
        self.grads, self.out, self.sems = grads, out, sems
        self.one, self.two, self.three, self.four = buffers
        width = grads.shape[-1]
        cut = width // 256 * 128
        self.first = pl.ds(0, cut or width)
        self.second = pl.ds(cut, width - cut) if cut else None
        z, x, c, y = place()
        self.peer_x = device(z, 1 - x, c, y)
        self.peer_y = device(z, x, c, 1 - y)
        self.peer_c = device(z, x, 1 - c, y)
        self.at = (z, x, c, y)
        self.copies = []
        self.pending = []

    @staticmethod
    def shapes(r, n):
        return [
            VMEM((4, 2, 2, r, n), BF16),
            VMEM((4, 2, r, n), BF16),
            VMEM((4, r, n), BF16),
            VMEM((3, r, n), BF16),
        ]

    def send(self, slot, peer, src, dst):
        copy = remote(src, dst, self.sems, slot, peer)
        copy.start()
        self.copies.append(copy)
        self.pending.append(copy)

    def land(self):
        for copy in self.pending:
            copy.wait_recv()
        self.pending = []

    def stage0(self):
        c = self.at[2]
        self.send(0, self.peer_c, self.grads.at[:, :, 1 - c], self.one)

    def stage1(self):
        z, x, c, y = self.at
        self.land()

        def add(i, carry):
            a, b = i // 2, i % 2
            self.one[a, b] = (
                self.one[a, b].astype(F32) + self.grads[a, b, c].astype(F32)
            ).astype(BF16)
            return carry

        lax.fori_loop(0, 8, add, 0)
        every = slice(None)
        self.send(
            1, self.peer_x, self.one.at[:, 1 - x, :, :, self.first],
            self.two.at[:, :, :, self.first],
        )
        if self.second is not None:
            self.send(
                2, self.peer_y, self.one.at[:, :, 1 - y, :, self.second],
                self.two.at[:, :, :, self.second],
            )

    def stage2(self):
        z, x, c, y = self.at
        self.land()

        def add(a, carry):
            cols = self.first
            self.two[a, :, :, cols] = (
                self.two[a, :, :, cols].astype(F32) + self.one[a, x, :, :, cols].astype(F32)
            ).astype(BF16)
            if self.second is not None:
                cols = self.second
                for b in range(2):
                    self.two[a, b, :, cols] = (
                        self.two[a, b, :, cols].astype(F32) + self.one[a, b, y, :, cols].astype(F32)
                    ).astype(BF16)
            return carry

        lax.fori_loop(0, 4, add, 0)
        self.send(
            3, self.peer_y, self.two.at[:, 1 - y, :, self.first], self.three.at[:, :, self.first]
        )
        if self.second is not None:
            self.send(
                4, self.peer_x, self.two.at[:, 1 - x, :, self.second],
                self.three.at[:, :, self.second],
            )

    def stage3(self):
        z, x, c, y = self.at
        self.land()

        def add(a, carry):
            for cols, which in ((self.first, y), (self.second, x)):
                if cols is not None:
                    self.three[a, :, cols] = (
                        self.three[a, :, cols].astype(F32) + self.two[a, which, :, cols].astype(F32)
                    ).astype(BF16)
            return carry

        lax.fori_loop(0, 4, add, 0)
        for d in (2, 1, 3):
            other = lax.rem(z + d, 4)
            self.send(4 + d, device(other, x, c, y), self.three.at[other], self.four.at[d - 1])

    def stage4(self):
        z = self.at[0]
        self.land()
        self.out[...] = (
            self.three[z].astype(F32)
            + self.four[0].astype(F32)
            + self.four[1].astype(F32)
            + self.four[2].astype(F32)
        )
        for copy in self.copies:
            copy.wait_send()


def fold(values, each, row):
    width = 32 * each
    shard = lax.broadcasted_iota(jnp.int32, (32, 16, width), 0)
    col = lax.broadcasted_iota(jnp.int32, (32, 16, width), 2)
    inside = (col >= shard * each) & (col < shard * each + each)
    spreaded = jnp.where(inside, values[None], 0.0).reshape(32 * 16, width).astype(BF16)
    lane = lax.broadcasted_iota(jnp.int32, (128, width), 0)
    col = lax.broadcasted_iota(jnp.int32, (128, width), 1)
    return nt(spreaded, (lax.rem(col, each) == lane).astype(BF16))


def scatter_kernel(count, *refs):
    grads = refs[:count]
    smalls = refs[count : count + 4]
    outs = refs[count + 4 : 2 * count + 5]
    buffers = refs[2 * count + 5 :]
    small_grads = buffers[0]
    buffers = buffers[1:]
    send, recv = buffers[-2:]
    greet()
    parts = []
    for i in range(count + 1):
        own = grads[i] if i < count else small_grads
        parts.append(Scatter(own, outs[i], buffers[4 * i : 4 * i + 4], (send.at[i], recv.at[i])))
    for part in parts[:-1]:
        part.stage0()
    total = fold(smalls[0][...] + smalls[1][...], 24, 0)
    total = total + fold(smalls[2][...], 72, 6) + fold(smalls[3][...], 96, 7)
    small_grads[...] = total.reshape(4, 2, 2, 2, 16, 128).astype(BF16)
    parts[-1].stage0()
    for stage in ("stage1", "stage2", "stage3", "stage4"):
        for part in parts:
            getattr(part, stage)()


def scatter_call(grads, smalls):
    inside = pl.BlockSpec(memory_space=VMEM)
    shapes = [g.shape[-2:] for g in grads] + [(16, 128)]
    scratch = [VMEM((4, 2, 2, 2, 16, 128), BF16)]
    for r, n in shapes:
        scratch += Scatter.shapes(r, n)
    scratch += [pltpu.SemaphoreType.DMA((len(shapes), Scatter.slots))] * 2
    return pl.pallas_call(
        functools.partial(scatter_kernel, len(grads)),
        out_shape=tuple(jax.ShapeDtypeStruct(s, F32) for s in shapes),
        in_specs=[inside] * (len(grads) + 4),
        out_specs=(inside,) * len(shapes),
        scratch_shapes=scratch,
        compiler_params=pltpu.CompilerParams(
            collective_id=2, has_side_effects=True, vmem_limit_bytes=60 * 2**20
        ),
    )(*grads, *smalls)


def shards(
    tokens, cotangent, lengths, ln1_gain, ln1_shift, qkv_weight, qkv_bias, out_weight, out_bias,
    ln2_gain, ln2_shift, up_weight, up_bias, down_weight, down_bias, *, special,
):
    vectors = (ln1_gain, ln1_shift, out_bias, ln2_gain, ln2_shift, down_bias, qkv_bias, up_bias)
    if special:
        small = jnp.stack(
            [jnp.pad(v, (0, 128 - v.shape[0])) for v in vectors] + [jnp.zeros((128,), BF16)] * 8
        )
        _, wqkv, wout, wup, wdown, vec24, vec72, vec96 = gather_call(
            small, qkv_weight, out_weight, up_weight, down_weight
        )
        wqkv, wout, wup = (w.reshape(D, w.shape[-1]) for w in (wqkv, wout, wup))
        wdown = wdown.reshape(FF, D)
    else:
        gather = functools.partial(lax.all_gather, axis_name=AXES, axis=0, tiled=True)
        wqkv, wout, wup, wdown = map(gather, (qkv_weight, out_weight, up_weight, down_weight))
        whole = [gather(v).astype(F32) for v in vectors]
        vec24 = jnp.pad(jnp.stack(whole[:6]), ((0, 10), (0, 0)))
        vec72 = jnp.pad(whole[6][None], ((6, 9), (0, 0)))
        vec96 = jnp.pad(whole[7][None], ((7, 8), (0, 0)))
    qkv, attended, lse = forward_call(tokens, vec24, vec72, wqkv)
    mixed, do, dy1, gout, gup, gdown, s24_mid, s96 = middle_call(
        lengths, tokens, attended, cotangent, vec24, vec96, wout, wup, wdown, 32
    )
    gx, gqkv, s24, s72 = backward_call(tokens, dy1, vec24, wqkv, qkv, attended, do, lse, 32)
    if special:
        blocks = [g.reshape(4, 2, 2, 2, *g.shape[1:]) for g in (gqkv, gout, gup, gdown)]
        gqkv, gout, gup, gdown, small = scatter_call(blocks, (s24, s24_mid, s72, s96))
        sizes = [v.shape[0] for v in vectors]
        folded = [small[i, :n] for i, n in enumerate(sizes)]
    else:
        scatter = functools.partial(
            lax.psum_scatter, axis_name=AXES, scatter_dimension=0, tiled=True
        )
        gqkv, gout, gup = (scatter(g.reshape(D, -1).astype(F32)) for g in (gqkv, gout, gup))
        gdown = scatter(gdown.reshape(FF, D).astype(F32))
        both = s24 + s24_mid
        folded = [scatter(both[i]) for i in range(6)] + [scatter(s72[6]), scatter(s96[7])]
    return (
        mixed, gx, folded[0], folded[1], gqkv, folded[6], gout, folded[2], folded[3], folded[4],
        gup, folded[7], gdown, folded[5],
    )


def solution(mesh):
    flat, rows = P(AXES), P(AXES, None)
    in_specs = (
        rows, rows, flat, flat, flat, rows, flat, rows, flat, flat, flat, rows, flat, rows, flat,
    )
    out_specs = (
        rows, rows, flat, flat, rows, flat, rows, flat, flat, flat, rows, flat, rows, flat,
    )
    special = dict(mesh.shape) == {"wide": 16, "narrow": 2}
    return jax.shard_map(
        functools.partial(shards, special=special),
        mesh=mesh, in_specs=in_specs, out_specs=out_specs, check_vma=False,
    )
```

time: 951 us -> 366 us (0.38); the launches traced: 939 us -> 366 us
  Pallas kernels: 0 us -> 341 us
  matrix products: 338 us -> 0 us
  waiting for transfers between devices: 319 us -> 0 us
  other arithmetic: 89.9 us -> 0 us
  blocking collectives: 85.4 us -> 0 us
  local copies, waits for them, and re-layouts: 90.3 us -> 23.6 us
  between operations: 15.6 us -> 1.34 us
    pallas_call x0 -> x5, Pallas kernels: none -> 341 us  [the longest x1 102 us: scatter_call(): pl.pallas_call(functools.partial(scatter_kernel, len(grads)), out_shape=t...]
    dot_general x96 -> x0, matrix products: 338 us -> none  [the longest x12 56.7 us: head_forward(): result = jnp.dot(weights, value_rows, preferred_element_type=jnp.float32)]
    reduce_scatter x4 -> x0, waiting for transfers between devices: 290 us -> none  [the longest x1 142 us: shards(): lax.psum_scatter(grad_down, ('wide', 'narrow'), scatter_dimension=0, tile...]
    unnamed x2 -> x0, blocking collectives: 85.4 us -> none
    convert_element_type x21 -> x0, other arithmetic: 63.7 us -> none  [the longest x12 58.2 us: head_backward(): grad_scores = jnp.where(causal, grad_scores, 0.0).astype(jnp.bfloat16)]
    while x27 -> x0, local copies, waits for them, and re-layouts: 34.3 us -> none
    all_gather x4 -> x0, waiting for transfers between devices: 26.4 us -> none  [the longest x1 16.9 us: shards(): lax.all_gather(down_weight, ('wide', 'narrow'), axis=0, tiled=True)]
    reduce_sum x19 -> x0, other arithmetic: 26 us -> none  [the longest x12 13.8 us: head_forward(): total = jnp.sum(expon, axis=1, keepdims=True)]
  transfers between devices with their start and end apart: 8 -> 0, of which waited for: 5 -> 0; matrix products, arithmetic and copies ran while one was open for 47% -> 0% of each run, Pallas kernels for 0% -> 0%
where the time goes in v1:
time: 366 us
  Pallas kernels  341 us (93%)
  local copies, waits for them, and re-layouts  23.6 us (6%)
    pallas_call x1, Pallas kernels, scatter_call(): pl.pallas_call(functools.partial(scatter_kernel, len(grads)), out_shape=t...  102 us
    pallas_call x1, Pallas kernels, gather_call(): pl.pallas_call(gather_kernel, out_shape=(*full, jax.ShapeDtypeStruct((16,...  93.7 us
    pallas_call x1, Pallas kernels, backward_call(): pl.pallas_call(backward_kernel, out_shape=(jax.ShapeDtypeStruct((length,...  55.8 us
    pallas_call x1, Pallas kernels, middle_call(): pl.pallas_call(middle_kernel, grid=(length // BLK,), out_shape=tuple((jax...  53.3 us
    pallas_call x1, Pallas kernels, forward_call(): pl.pallas_call(forward_kernel, out_shape=(jax.ShapeDtypeStruct((length, 3...  36.3 us
    unnamed x24, local copies, waits for them, and re-layouts  17 us

profile of v1, /device:TPU:0, one launch (start us, length us, event | category | flops | bytes accessed | tf_op | source)
XLA Modules:
  0.0 365.9 jit_solution(277395373110495772)
XLA Ops:
  1.3 0.7 pad_bitcast_fusion.6
  2.0 0.7 pad_bitcast_fusion
  2.6 0.7 pad_bitcast_fusion.4
  3.3 0.7 pad_bitcast_fusion.2
  4.0 0.0 copy-start.5
  4.0 0.9 copy-done.5
  5.0 0.0 copy-start.6
  5.0 0.9 copy-done.6
  5.9 0.0 copy-start.8
  5.9 0.9 copy-done.8
  6.8 0.0 copy-start.9
  6.8 0.8 copy-done.9
  7.5 93.7 %shard_map.254 = (bf16[4,2,2,2,16,128]{5,4,3,2,1,0:T(8,128)(2,1)}, bf16[4,2,2,2,24,2304]{5,4,3,2,1,0:T(8,128)(2,1)S(1)}, bf16[4,2,2,2,24,768]{5,4,3,2,1,0:T(8,12...) custom-call(bf16[16,128]{1,0:T(8,128)(2,1)S(1)} %stack.39.small, ...), custom_call_target="tpu_custom_call" | custom-call | tf_op jit(solution)/shard_map/pallas_call | solution.py:523
  101.3 0.0 copy-start
  101.3 1.8 copy-done
  103.1 0.0 copy-start.1
  103.1 2.2 copy-done.1
  105.3 1.0 copy-done.2
  106.3 0.6 copy-done.3
  107.0 0.7 copy-done.4
  107.6 0.7 copy-done.7
  108.3 36.3 %shard_map.255 = (bf16[1024,2304]{1,0:T(8,128)(2,1)}, bf16[1024,768]{1,0:T(8,128)(2,1)}, f32[6,8,1024]{2,1,0:T(8,128)}) custom-call(bf16[1024,768]{1,0:T(8,128)(2,1)} %x_ref.5, f32[16,768]{1,0:T(8,128)} %copy-done.3, f32[16,2304]{1,0:T(8,128)} %copy-done.7, bf16[768,2304]{1,0:T(8,128)(2,1)} %bitcast.40), custom_call_target="tpu_custom_call" | custom-call | tf_op jit(solution)/shard_map/pallas_call | solution.py:160
  144.6 53.3 %shard_map.256 = (bf16[1024,768]{1,0:T(8,128)(2,1)}, bf16[1024,768]{1,0:T(8,128)(2,1)}, f32[1024,768]{1,0:T(8,128)}, bf16[32,24,768]{2,1,0:T(8,128)(2,1)}, bf16[...) custom-call(s32[1]{0:T(128)S(6)} %copy.33.len_ref, ...), custom_call_target="tpu_custom_call" | custom-call | tf_op jit(solution)/shard_map/pallas_call | solution.py:284
  198.0 55.8 %shard_map.257 = (bf16[1024,768]{1,0:T(8,128)(2,1)}, bf16[32,24,2304]{2,1,0:T(8,128)(2,1)}, f32[16,768]{1,0:T(8,128)}, f32[16,2304]{1,0:T(8,128)}) custom-call(bf16[1024,768]{1,0:T(8,128)(2,1)} %x_ref.5, f32[1024,768]{1,0:T(8,128)} %get-tuple-element.50.dy1_ref, f32[16,768]{1,0:T(8,128)} %copy-done.3, bf16[768,2304]{1,0:T(8,128)(2,1)} %bitcast.41, ...), custom_call_target="tpu_custom_call" | custom-call | tf_op jit(solution)/shard_map/pallas_call | solution.py:366
  253.7 101.8 %shard_map.258 = (f32[24,2304]{1,0:T(8,128)}, f32[24,768]{1,0:T(8,128)}, f32[24,3072]{1,0:T(8,128)}, f32[96,768]{1,0:T(8,128)}, f32[16,128]{1,0:T(8,128)}) custom-call(bf16[4,2,2,2,24,2304]{5,4,3,2,1,0:T(8,128)(2,1)} %bitcast.47, bf16[4,2,2,2,24,768]{5,4,3,2,1,0:T(8,128)(2,1)} %bitcast.48, bf16[4,2,2,2,24,3072]{5,4,3,2,1,0:T(8,128)(2,1)} %bitcast.44, ...), custom_call_target="tpu_custom_call" | custom-call | tf_op jit(solution)/shard_map/pallas_call | solution.py:708
  355.6 1.2 slice_bitcast_fusion.5
  356.7 1.2 slice_bitcast_fusion.1
  357.9 1.4 slice_bitcast_fusion
  359.3 1.6 copy.34
  361.0 1.5 copy.35
  362.5 1.7 copy.36
  364.2 1.7 copy.37
  (6 shorter events, 0.1 us)
Async XLA Ops:
  4.0 0.9 copy-start.5
  5.0 0.9 copy-start.6
  5.9 0.9 copy-start.8
  6.8 0.8 copy-start.9
  101.3 1.8 copy-start
  103.1 2.2 copy-start.1
  105.3 1.0 copy-start.2
  106.3 0.6 copy-start.3
  107.0 0.7 copy-start.4
  107.6 0.7 copy-start.7

commit v2 on v1

v2 whole, which is shorter than its diff:
```python
import functools

import jax
import jax.numpy as jnp
from jax import lax
from jax.experimental import pallas as pl
from jax.experimental.pallas import tpu as pltpu
from jax.sharding import PartitionSpec as P

D = 768
FF = 3072
HEADS = 12
HEAD = 64
BLK = 256
MID = 256
CHUNK = 768
AXES = ("wide", "narrow")
MESH = pl.DeviceIdType.MESH
VMEM = pltpu.VMEM
F32 = jnp.float32
BF16 = jnp.bfloat16


def nn(left, right):
    return lax.dot_general(left, right, (((1,), (0,)), ((), ())), preferred_element_type=F32)


def nt(left, right):
    return lax.dot_general(left, right, (((1,), (1,)), ((), ())), preferred_element_type=F32)


def norm_parts(values):
    average = jnp.mean(values, axis=-1, keepdims=True)
    centered = values - average
    inverse = lax.rsqrt(jnp.mean(centered * centered, axis=-1, keepdims=True) + 1e-05)
    return centered * inverse, inverse


def norm_back(grad_normed, normed, inverse):
    first_mean = jnp.mean(grad_normed, axis=-1, keepdims=True)
    second_mean = jnp.mean(grad_normed * normed, axis=-1, keepdims=True)
    return inverse * (grad_normed - first_mean - normed * second_mean)


def lane_half(values, half):
    lanes = lax.broadcasted_iota(jnp.int32, values.shape, 1)
    keep = (lanes < HEAD) if half == 0 else (lanes >= HEAD)
    return jnp.where(keep, values, jnp.zeros_like(values))


def diagonal_keep():
    keys = lax.broadcasted_iota(jnp.int32, (BLK, BLK), 0)
    queries = lax.broadcasted_iota(jnp.int32, (BLK, BLK), 1)
    return keys <= queries


def column(pair, part):
    return pl.ds(pl.multiple_of(part * D + pair * 128, 128), 128)


def qkv_rows(block, x_ref, vec24_ref, vec72_ref, wqkv_ref, qkv_ref):
    rows = pl.ds(pl.multiple_of(block * BLK, BLK), BLK)
    normed, _ = norm_parts(x_ref[rows, :].astype(F32))
    hidden = (normed * vec24_ref[0:1, :] + vec24_ref[1:2, :]).astype(BF16)
    for part in range(3):
        cols = slice(part * D, (part + 1) * D)
        qkv_ref[rows, cols] = (nn(hidden, wqkv_ref[:, cols]) + vec72_ref[6:7, cols]).astype(BF16)


def attention_pair(pair, qkv_ref, o_ref, lse_ref, vt, event=lambda j: None):
    length = qkv_ref.shape[0]
    vt[...] = qkv_ref[:, column(pair, 2)].T
    keep = diagonal_keep()
    for j in range(length // BLK):
        event(j)
        span = (j + 1) * BLK
        rows = slice(j * BLK, span)
        query = qkv_ref[rows, column(pair, 0)] * jnp.asarray(0.125, BF16)
        keys = qkv_ref[0:span, column(pair, 1)]
        outs = []
        for half in range(2):
            s = nt(keys, lane_half(query, half))
            w = s * s + 1.0
            m = w * lax.rsqrt(w)
            tail = jnp.where(keep, m[j * BLK :], -1e30)
            m = tail if j == 0 else jnp.concatenate([m[: j * BLK], tail], axis=0)
            top = jnp.max(m, axis=0, keepdims=True)
            e = jnp.exp(m - top)
            total = jnp.sum(e, axis=0, keepdims=True)
            a = (jnp.tanh(s) * e).astype(BF16)
            outs.append(nn(vt[half * HEAD : (half + 1) * HEAD, 0:span], a) / total)
            lse_ref[pair, half : half + 1, rows] = top + jnp.log(total)
        o_ref[rows, column(pair, 0)] = jnp.concatenate(outs, axis=0).T.astype(BF16)


def attention_back_pair(
    pair, qkv_ref, o_ref, do_ref, lse_ref, dqkv_ref, kt, dk, dv, event=lambda j: None
):
    length = qkv_ref.shape[0]
    kt[...] = qkv_ref[:, column(pair, 1)].T
    keep = diagonal_keep()
    lanes = lax.broadcasted_iota(jnp.int32, (8, 128), 1)
    sublanes = lax.broadcasted_iota(jnp.int32, (8, 128), 0)
    pick = (lanes // HEAD == sublanes).astype(F32)
    steps = length // BLK
    for j in reversed(range(steps)):
        event(j)
        span = (j + 1) * BLK
        rows = slice(j * BLK, span)
        query = qkv_ref[rows, column(pair, 0)] * jnp.asarray(0.125, BF16)
        grad = do_ref[rows, column(pair, 0)]
        product = grad.astype(F32) * o_ref[rows, column(pair, 0)].astype(F32)
        inner = lax.dot_general(
            pick, product, (((1,), (1,)), ((), ())),
            precision=lax.Precision.HIGHEST, preferred_element_type=F32,
        )
        keys = qkv_ref[0:span, column(pair, 1)]
        values = qkv_ref[0:span, column(pair, 2)]
        dqs = []
        dks = None
        dvs = None
        for half in range(2):
            query_half = lane_half(query, half)
            grad_half = lane_half(grad, half)
            s = nt(keys, query_half)
            da = nt(values, grad_half)
            w = s * s + 1.0
            r = lax.rsqrt(w)
            p = jnp.exp(w * r - lse_ref[pair, half : half + 1, rows])
            tail = jnp.where(keep, p[j * BLK :], 0.0)
            p = tail if j == 0 else jnp.concatenate([p[: j * BLK], tail], axis=0)
            t = jnp.tanh(s)
            a = (t * p).astype(BF16)
            ds = p * (da * (1.0 - t * t) + (da * t - inner[half : half + 1, :]) * (s * r))
            ds = ds.astype(BF16)
            dqs.append(nn(kt[half * HEAD : (half + 1) * HEAD, 0:span], ds))
            this_dk = nn(ds, query_half)
            this_dv = nn(a, grad_half)
            dks = this_dk if half == 0 else dks + this_dk
            dvs = this_dv if half == 0 else dvs + this_dv
        dqkv_ref[rows, column(pair, 0)] = (jnp.concatenate(dqs, axis=0).T * 0.125).astype(BF16)
        if j == steps - 1:
            dk[...] = dks
            dv[...] = dvs
        else:
            dk[0:span, :] += dks
            dv[0:span, :] += dvs
    dqkv_ref[:, column(pair, 1)] = dk[...].astype(BF16)
    dqkv_ref[:, column(pair, 2)] = dv[...].astype(BF16)


def forward_kernel(x_ref, vec24_ref, vec72_ref, wqkv_ref, qkv_ref, o_ref, lse_ref, vt):
    lax.fori_loop(
        0,
        x_ref.shape[0] // BLK,
        lambda b, c: (qkv_rows(b, x_ref, vec24_ref, vec72_ref, wqkv_ref, qkv_ref), c)[1],
        0,
    )
    lax.fori_loop(
        0, HEADS // 2, lambda p, c: (attention_pair(p, qkv_ref, o_ref, lse_ref, vt), c)[1], 0
    )


def forward_call(x, vec24, vec72, wqkv):
    length = x.shape[0]
    return pl.pallas_call(
        forward_kernel,
        out_shape=(
            jax.ShapeDtypeStruct((length, 3 * D), BF16),
            jax.ShapeDtypeStruct((length, D), BF16),
            jax.ShapeDtypeStruct((HEADS // 2, 8, length), F32),
        ),
        in_specs=[pl.BlockSpec(memory_space=VMEM)] * 4,
        out_specs=(pl.BlockSpec(memory_space=VMEM),) * 3,
        scratch_shapes=[VMEM((128, length), BF16)],
        compiler_params=pltpu.CompilerParams(vmem_limit_bytes=56 * 2**20),
    )(x, vec24, vec72, wqkv)


def middle_kernel(
    len_ref, x_ref, o_ref, cot_ref, vec24_ref, vec96_ref, wout_all, wup_all, wdown_all,
    mixed_ref, do_ref, dy1_ref, gout_ref, gup_ref, gdown_ref, small24_ref, small96_ref,
    f_t, du, h2_t, dy, dz, o_t, wout_ref, wup_ref, wdown_ref, flat, load, store,
):
    step = pl.program_id(0)
    steps = pl.num_programs(0)
    rows_at = pl.multiple_of(step * MID, MID)
    here = pl.ds(rows_at, MID)
    chunk = 768
    weights = ((wout_all, wout_ref), (wup_all, wup_ref), (wdown_all, wdown_ref))
    loads = [pltpu.make_async_copy(a, b, load.at[i]) for i, (a, b) in enumerate(weights)]

    @pl.when(step == 0)
    def _():
        for copy in loads:
            copy.start()
        small24_ref[...] = jnp.zeros_like(small24_ref)
        small96_ref[...] = jnp.zeros_like(small96_ref)
        loads[0].wait()

    attended = o_ref[...]
    y1 = x_ref[...].astype(F32) + nn(attended, wout_ref[...]) + vec24_ref[2:3, :]
    normed, inverse = norm_parts(y1)
    h2 = (normed * vec24_ref[3:4, :] + vec24_ref[4:5, :]).astype(BF16)
    rows = lax.broadcasted_iota(jnp.int32, (MID, D), 0) + rows_at
    upstream = jnp.where(rows < len_ref[0], cot_ref[...].astype(F32), 0.0)
    upstream16 = upstream.astype(BF16)
    h2_t[:, here] = h2.T
    o_t[:, here] = attended.T
    dy[here, :] = upstream16
    small24_ref[5:6, :] += jnp.sum(upstream, axis=0, keepdims=True)

    @pl.when(step == 0)
    def _():
        loads[1].wait()
        loads[2].wait()

    y = y1 + vec24_ref[5:6, :]
    dh2 = None
    for c in range(FF // CHUNK):
        cols = slice(c * CHUNK, (c + 1) * CHUNK)
        u = nn(h2, wup_ref[:, cols]) + vec96_ref[7:8, cols]
        square = u * u
        t = jnp.tanh(u * (0.7978845608028654 + 0.035677408136300125 * square))
        half = 0.5 * (1.0 + t)
        f = (u * half).astype(BF16)
        slope = half + (0.5 * u) * (1.0 - t * t) * (
            0.7978845608028654 + 0.10703222440890037 * square
        )
        y = y + nn(f, wdown_ref[cols, :])
        df = nt(upstream16, wdown_ref[cols, :])
        d16 = (df * slope).astype(BF16)
        du[here, cols] = d16
        f_t[cols, here] = f.T
        small96_ref[7:8, cols] += jnp.sum(d16.astype(F32), axis=0, keepdims=True)
        part = nt(d16, wup_ref[:, cols])
        dh2 = part if c == 0 else dh2 + part
    mixed_ref[...] = y.astype(BF16)
    e = dh2 * vec24_ref[3:4, :]
    dy1 = dy[here, :].astype(F32) + norm_back(e, normed, inverse)
    dz16 = dy1.astype(BF16)
    dy1_ref[...] = dy1
    do_ref[...] = nt(dz16, wout_ref[...]).astype(BF16)
    small24_ref[2:3, :] += jnp.sum(dz16.astype(F32), axis=0, keepdims=True)
    small24_ref[3:4, :] += jnp.sum(dh2 * normed, axis=0, keepdims=True)
    small24_ref[4:5, :] += jnp.sum(dh2, axis=0, keepdims=True)
    dz[here, :] = dz16

    @pl.when(step == steps - 1)
    def _():
        shards = gout_ref.shape[0]

        def pipeline(count, stage, compute, target):
            def one(k, carry):
                slot = lax.rem(k, 2)
                copy = pltpu.make_async_copy(stage.at[slot], target(k), store.at[slot])

                @pl.when(k >= 2)
                def _():
                    copy.wait()

                stage[slot] = compute(k)
                copy.start()
                return carry

            lax.fori_loop(0, count, one, 0)
            for k in (count - 2, count - 1):
                pltpu.make_async_copy(stage.at[k % 2], target(k), store.at[k % 2]).wait()

        def blocks(value, depth):
            return value.reshape(value.shape[0] // depth, depth, value.shape[1]).astype(BF16)

        def block(k):
            return pl.ds(pl.multiple_of(k * chunk, chunk), chunk)

        pipeline(
            4,
            flat,
            lambda k: blocks(nn(f_t[block(k), :], dy[...]), D // shards),
            lambda k: gdown_ref.at[pl.ds(k * shards, shards)],
        )
        pipeline(
            4,
            flat,
            lambda k: blocks(nn(h2_t[...], du[:, block(k)]), D // shards),
            lambda k: gup_ref.at[:, :, block(k)],
        )
        flat[0] = blocks(nn(o_t[...], dz[...]), D // shards)
        last = pltpu.make_async_copy(flat.at[0], gout_ref, store.at[0])
        last.start()
        last.wait()


def middle_call(lengths, x, attended, cotangent, vec24, vec96, wout, wup, wdown, shards):
    length = x.shape[0]

    def rows(width):
        return pl.BlockSpec((MID, width), lambda i: (i, 0))

    def whole(shape):
        return pl.BlockSpec(shape, lambda i: (0,) * len(shape), pipeline_mode=pl.Buffered(1))

    anywhere = pl.BlockSpec(memory_space=pl.ANY)
    outs = (
        ((length, D), BF16, rows(D)),
        ((length, D), BF16, rows(D)),
        ((length, D), F32, rows(D)),
        ((shards, D // shards, D), BF16, anywhere),
        ((shards, D // shards, FF), BF16, anywhere),
        ((FF // D * shards, D // shards, D), BF16, anywhere),
        ((16, D), F32, whole((16, D))),
        ((16, FF), F32, whole((16, FF))),
    )
    return pl.pallas_call(
        middle_kernel,
        grid=(length // MID,),
        out_shape=tuple(jax.ShapeDtypeStruct(s, t) for s, t, _ in outs),
        in_specs=[
            pl.BlockSpec(memory_space=pltpu.SMEM),
            rows(D), rows(D), rows(D),
            whole(vec24.shape), whole(vec96.shape),
            anywhere, anywhere, anywhere,
        ],
        out_specs=tuple(b for _, _, b in outs),
        scratch_shapes=[
            VMEM((FF, length), BF16),
            VMEM((length, FF), BF16),
            VMEM((D, length), BF16),
            VMEM((length, D), BF16),
            VMEM((length, D), BF16),
            VMEM((D, length), BF16),
            VMEM(wout.shape, BF16),
            VMEM(wup.shape, BF16),
            VMEM(wdown.shape, BF16),
            VMEM((2, shards, D // shards, D), BF16),
            pltpu.SemaphoreType.DMA((3,)),
            pltpu.SemaphoreType.DMA((2,)),
        ],
        compiler_params=pltpu.CompilerParams(
            dimension_semantics=("arbitrary",), vmem_limit_bytes=63 * 2**20
        ),
    )(lengths, x, attended, cotangent, vec24, vec96, wout, wup, wdown)


def tail_rows(block, x_ref, dy1_ref, vec24_ref, wqkv_ref, dqkv_ref, h1_t, gx_ref, s24_ref, s72_ref):
    here = pl.ds(pl.multiple_of(block * BLK, BLK), BLK)
    normed, inverse = norm_parts(x_ref[here, :].astype(F32))
    if h1_t is not None:
        h1_t[:, here] = (normed * vec24_ref[0:1, :] + vec24_ref[1:2, :]).astype(BF16).T
    grad = dqkv_ref[here, :]
    dh1 = nt(grad, wqkv_ref[...])
    e = dh1 * vec24_ref[0:1, :]
    gx_ref[here, :] = (dy1_ref[here, :] + norm_back(e, normed, inverse)).astype(BF16)
    s24_ref[0:1, :] += jnp.sum(dh1 * normed, axis=0, keepdims=True)
    s24_ref[1:2, :] += jnp.sum(dh1, axis=0, keepdims=True)
    s72_ref[6:7, :] += jnp.sum(grad.astype(F32), axis=0, keepdims=True)


def backward_kernel(
    x_ref, dy1_ref, vec24_ref, wqkv_ref, qkv_ref, o_ref, do_ref, lse_ref,
    gx_ref, gqkv_ref, s24_ref, s72_ref,
    dqkv, h1_t, kt, dk, dv,
):
    s24_ref[...] = jnp.zeros_like(s24_ref)
    s72_ref[...] = jnp.zeros_like(s72_ref)
    lax.fori_loop(
        0,
        HEADS // 2,
        lambda p, c: (
            attention_back_pair(p, qkv_ref, o_ref, do_ref, lse_ref, dqkv, kt, dk, dv),
            c,
        )[1],
        0,
    )
    lax.fori_loop(
        0,
        x_ref.shape[0] // BLK,
        lambda b, c: (
            tail_rows(
                b, x_ref, dy1_ref, vec24_ref, wqkv_ref, dqkv, h1_t, gx_ref, s24_ref, s72_ref
            ),
            c,
        )[1],
        0,
    )
    shards = gqkv_ref.shape[0]
    many = shards // 4

    def one(i, carry):
        left = pl.ds(pl.multiple_of(i * (D // 4), D // 4), D // 4)
        for part in range(3):
            cols = slice(part * D, (part + 1) * D)
            value = nn(h1_t[left, :], dqkv[:, cols]).reshape(many, D // shards, D)
            gqkv_ref[pl.ds(i * many, many), :, cols] = value.astype(BF16)
        return carry

    lax.fori_loop(0, 4, one, 0)


def backward_call(x, dy1, vec24, wqkv, qkv, attended, grad_attended, lse, shards):
    length = x.shape[0]
    return pl.pallas_call(
        backward_kernel,
        out_shape=(
            jax.ShapeDtypeStruct((length, D), BF16),
            jax.ShapeDtypeStruct((shards, D // shards, 3 * D), BF16),
            jax.ShapeDtypeStruct((16, D), F32),
            jax.ShapeDtypeStruct((16, 3 * D), F32),
        ),
        in_specs=[pl.BlockSpec(memory_space=VMEM)] * 8,
        out_specs=(pl.BlockSpec(memory_space=VMEM),) * 4,
        scratch_shapes=[
            VMEM((length, 3 * D), BF16),
            VMEM((D, length), BF16),
            VMEM((128, length), BF16),
            VMEM((length, 128), F32),
            VMEM((length, 128), F32),
        ],
        compiler_params=pltpu.CompilerParams(vmem_limit_bytes=60 * 2**20),
    )(x, dy1, vec24, wqkv, qkv, attended, grad_attended, lse)


def place():
    wide = lax.axis_index("wide")
    return wide // 4, (wide // 2) % 2, wide % 2, lax.axis_index("narrow")


def device(z, x, c, y):
    return ((z * 2 + x) * 2 + c, y)


def greet():
    z, x, c, y = place()
    barrier = pltpu.get_barrier_semaphore()
    peers = [device(lax.rem(z + d, 4), x, c, y) for d in (1, 2, 3)]
    peers += [device(z, 1 - x, c, y), device(z, x, c, 1 - y), device(z, x, 1 - c, y)]
    for peer in peers:
        pl.semaphore_signal(barrier, inc=1, device_id=peer, device_id_type=MESH)
    pl.semaphore_wait(barrier, len(peers))


def remote(src, dst, sems, slot, peer):
    return pltpu.make_async_remote_copy(
        src_ref=src, dst_ref=dst, send_sem=sems[0].at[slot], recv_sem=sems[1].at[slot],
        device_id=peer, device_id_type=MESH,
    )


FIRST_Z = (("z", "x", "y"), ("z", "y", "x"))
LATER_Z = (("x", "z", "y"), ("y", "z", "x"))
UP_ORDERS = FIRST_Z
DOWN_ORDERS = LATER_Z


def peers_of(z, x, c, y):
    return {
        "z": [device(lax.rem(z + d, 4), x, c, y) for d in (1, 2, 3)],
        "x": [device(z, 1 - x, c, y)],
        "y": [device(z, x, c, 1 - y)],
        "c": [device(z, x, 1 - c, y)],
    }


def halves(low, high):
    cut = (high - low) // 256 * 128
    return [(low, low + cut), (low + cut, high)] if cut else [(low, high)]


def window(span):
    return pl.ds(span[0], span[1] - span[0])


class Gather:
    slots = 16

    def __init__(self, own, full, sems, local, rows=None, cols=None, orders=FIRST_Z):
        height, width = full.shape[-2:]
        span = cols or (0, width)
        rows = slice(None) if rows is None else window(rows)
        z, x, c, y = place()
        here = {"z": z, "x": x, "y": y}
        peers = peers_of(z, x, c, y)
        lanes = list(zip(halves(*span), orders))
        self.groups = [[], [], []]
        self.core = [[], [], [], []]
        slot = 0

        def at(state, cols):
            return full.at[state["z"], state["x"], c, state["y"], rows, window(cols)]

        for k in range(3):
            items = lanes
            if k == 0 and all(order[0] == orders[0][0] for _, order in lanes):
                items = [(span, orders[0])]
            for cols, order in items:
                now = {d: slice(None) if d in order[:k] else here[d] for d in "zxy"}
                source = own.at[rows, window(cols)] if k == 0 else at(now, cols)
                for peer in peers[order[k]]:
                    self.groups[k].append(remote(source, at(now, cols), sems, slot, peer))
                    slot += 1
                if "z" in order[: k + 1]:
                    later = dict(now)
                    later[order[k]] = slice(None) if order[k] == "z" else 1 - here[order[k]]
                    view = at(later, cols)
                    self.core[k + 1].append(remote(view, view, sems, slot, peers["c"][0]))
                    slot += 1
        self.kept = pltpu.make_async_copy(own.at[rows, window(span)], at(here, span), local)

    def run(self, stage):
        if stage == 0:
            self.kept.start()
        elif stage == 1:
            self.kept.wait()
        if 1 <= stage <= 3:
            for copy in self.groups[stage - 1]:
                copy.wait_recv()
        if stage <= 2:
            for copy in self.groups[stage]:
                copy.start()
        if stage <= 3:
            for copy in self.core[stage]:
                copy.start()
        every_core = [copy for copies in self.core for copy in copies]
        if stage == 4:
            for copy in every_core:
                copy.wait_recv()
        if stage == 5:
            for copy in every_core + [copy for copies in self.groups for copy in copies]:
                copy.wait_send()


def spread(blocks, each):
    width = 32 * each
    lane = lax.broadcasted_iota(jnp.int32, (128, width), 0)
    col = lax.broadcasted_iota(jnp.int32, (128, width), 1)
    value = nn(blocks, (lax.rem(col, each) == lane).astype(BF16)).reshape(32, 16, width)
    shard = lax.broadcasted_iota(jnp.int32, (32, 16, width), 0)
    col = lax.broadcasted_iota(jnp.int32, (32, 16, width), 2)
    inside = (col >= shard * each) & (col < shard * each + each)
    return jnp.sum(jnp.where(inside, value, 0.0), axis=0)


FORWARD = {
    "n": ("X0", "S0", "Y0",),
    "h": ("Z0", "X1", "S1", "O0", "X2", "U0", "S2", "Y1", "D0", "X3", "S3", "S4", "Y2",),
    0: ("X4", "Z1", "V0", "O1", "E0",),
    1: ("Y3", "Z2",),
    3: ("O2",),
    5: ("Z3", "U1", "D1",),
    8: ("O3",),
    9: ("V1",),
    10: ("Y4", "U2",),
    14: ("V2", "E1",),
    15: ("U3",),
    20: ("Z4", "D2",),
    21: ("V3",),
    24: ("E2",),
    25: ("D3",),
    "last": ("E3", "O4", "U4", "D4", "V4", "E4",),
}


def runner(parts, table):
    def run(at):
        for word in table.get(at, ()):
            parts[word[0]].run(int(word[1]))

    return run


def when_run(run, table, value, positions):
    for number, at in positions:
        if at in table:

            @pl.when(value == number)
            def _():
                run(at)


def gather_forward_kernel(
    x_ref, small_ref, wqkv_own, wout_own, wup_own, wdown_own,
    wqkv_out, wout_full, wup_full, wdown_full, vec24_ref, vec96_ref, qkv_out, o_out, lse_ref,
    small_full, wqkv_full, vec72, own_groups, hidden, vt, wqkv_ref, qkv_ref, o_ref,
    send, recv, local, store,
):
    greet()
    results = ((wqkv_ref, wqkv_out), (qkv_ref, qkv_out), (o_ref, o_out))
    stores = [pltpu.make_async_copy(a, b, store.at[i]) for i, (a, b) in enumerate(results)]
    length = x_ref.shape[0]
    steps = length // BLK
    half = wdown_full.shape[-2] // 2
    parts = {}

    def add_part(name, own, full, **view):
        i = len(parts)
        parts[name] = Gather(own, full, (send.at[i], recv.at[i]), local.at[i], **view)

    add_part("S", small_ref, small_full)
    for group, name in enumerate("XYZ"):
        add_part(name, own_groups, wqkv_full, cols=(group * D, (group + 1) * D))
        for part in range(3):
            own_groups[:, (3 * group + part) * 256 : (3 * group + part + 1) * 256] = wqkv_own[
                :, part * D + group * 256 : part * D + (group + 1) * 256
            ]
    add_part("O", wout_own, wout_full)
    add_part("U", wup_own, wup_full, cols=(0, FF // 2), orders=UP_ORDERS)
    add_part("V", wup_own, wup_full, cols=(FF // 2, FF), orders=UP_ORDERS)
    add_part("D", wdown_own, wdown_full, rows=(0, half), orders=DOWN_ORDERS)
    add_part("E", wdown_own, wdown_full, rows=(half, 2 * half), orders=DOWN_ORDERS)
    run = runner(parts, FORWARD)
    run("n")

    def normalize(block, carry):
        here = pl.ds(pl.multiple_of(block * BLK, BLK), BLK)
        normed, _ = norm_parts(x_ref[here, :].astype(F32))
        hidden[here, :] = (normed * vec24_ref[0:1, :] + vec24_ref[1:2, :]).astype(BF16)
        return carry

    run("h")
    blocks = small_full[...].reshape(32 * 16, 128)
    for ref, each in zip((vec24_ref, vec72, vec96_ref), (24, 72, 96)):
        ref[...] = spread(blocks, each)
    lax.fori_loop(0, steps, normalize, 0)

    def group_qkv(group):
        wide = pl.ds(pl.multiple_of(group * D, D), D)

        def spot(part):
            return pl.ds(pl.multiple_of(part * D + group * 256, 256), 256)

        def flatten(i, carry):
            two = wqkv_full[i // 4, (i // 2) % 2, i % 2, :, :, wide].astype(F32)
            two = two.reshape(D // 16, D).astype(BF16)
            rows = pl.ds(pl.multiple_of(i * (D // 16), D // 16), D // 16)
            for part in range(3):
                wqkv_ref[rows, spot(part)] = two[:, part * 256 : (part + 1) * 256]
            return carry

        lax.fori_loop(0, 16, flatten, 0)

        def rows_qkv(block, carry):
            here = pl.ds(pl.multiple_of(block * BLK, BLK), BLK)
            for part in range(3):
                value = nn(hidden[here, :], wqkv_ref[:, spot(part)]) + vec72[6:7, spot(part)]
                qkv_ref[here, spot(part)] = value.astype(BF16)
            return carry

        lax.fori_loop(0, steps, rows_qkv, 0)

    def one(pair, carry):
        def event(j):
            spots = [(p, p * (steps + 1) + 1 + j) for p in range(HEADS // 2)]
            when_run(run, FORWARD, pair, spots)

        event(-1)

        @pl.when(pair % 2 == 0)
        def _():
            group_qkv(pair // 2)

        attention_pair(pair, qkv_ref, o_ref, lse_ref, vt, event)
        return carry

    lax.fori_loop(0, HEADS // 2, one, 0)
    for copy in stores:
        copy.start()
    run("last")
    for part in parts.values():
        part.run(5)
    for copy in stores:
        copy.wait()


def gather_forward_call(x, small, wqkv, wout, wup, wdown):
    length = x.shape[0]
    anywhere = pl.BlockSpec(memory_space=pl.ANY)
    inside = pl.BlockSpec(memory_space=VMEM)

    def full(own):
        return jax.ShapeDtypeStruct((4, 2, 2, 2, *own.shape), BF16)

    return pl.pallas_call(
        gather_forward_kernel,
        out_shape=(
            jax.ShapeDtypeStruct((D, 3 * D), BF16),
            full(wout), full(wup), full(wdown),
            jax.ShapeDtypeStruct((16, D), F32),
            jax.ShapeDtypeStruct((16, FF), F32),
            jax.ShapeDtypeStruct((length, 3 * D), BF16),
            jax.ShapeDtypeStruct((length, D), BF16),
            jax.ShapeDtypeStruct((HEADS // 2, 8, length), F32),
        ),
        in_specs=[inside] * 3 + [anywhere] * 3,
        out_specs=(*[anywhere] * 4, inside, inside, anywhere, anywhere, inside),
        scratch_shapes=[
            VMEM((4, 2, 2, 2, 16, 128), BF16),
            VMEM((4, 2, 2, 2, *wqkv.shape), BF16),
            VMEM((16, 3 * D), F32),
            VMEM(wqkv.shape, BF16),
            VMEM((length, D), BF16),
            VMEM((128, length), BF16),
            VMEM((D, 3 * D), BF16),
            VMEM((length, 3 * D), BF16),
            VMEM((length, D), BF16),
            pltpu.SemaphoreType.DMA((9, Gather.slots)),
            pltpu.SemaphoreType.DMA((9, Gather.slots)),
            pltpu.SemaphoreType.DMA((9,)),
            pltpu.SemaphoreType.DMA((3,)),
        ],
        compiler_params=pltpu.CompilerParams(
            collective_id=1, has_side_effects=True, vmem_limit_bytes=60 * 2**20
        ),
    )(x, small, wqkv, wout, wup, wdown)


SIZES = {"z": 4, "x": 2, "y": 2}


def held_after(order, k):
    return [d for d in "zxy" if d not in order[:k]]


class Scatter:
    slots = 12

    def __init__(self, grads, buffers, sems, local, put, rows=None, cols=None, orders=FIRST_Z):
        height, width = grads.shape[-2:]
        low, high = cols or (0, width)
        rows = slice(None) if rows is None else window(rows)
        cols = slice(None) if cols is None else window(cols)
        z, x, c, y = place()
        self.here = {"z": z, "x": x, "y": y}
        self.core_at = c
        peers = peers_of(z, x, c, y)
        self.grads, self.put = grads, put
        self.mine, self.one, *rest = buffers
        if self.mine is not None:
            self.kept = pltpu.make_async_copy(grads.at[:, :, c, :, rows, cols], self.mine, local)
        self.groups = [[remote(grads.at[:, :, 1 - c, :, rows, cols], self.one, sems, 0, peers["c"][0])]]
        self.groups += [[], [], []]
        self.lanes = []
        slot = 1
        for span, order in zip(halves(0, high - low), orders):
            order = order[::-1]
            got = [rest.pop(0) for _ in range(3)]
            self.lanes.append((window(span), order, got))
            for k in range(3):
                source = self.one if k == 0 else got[k - 1]
                cut = (slice(None), window(span)) if k == 0 else (slice(None), slice(None))
                if k > 0 and order[k - 1] == "z":
                    source = source.at[0]
                if order[k] == "z":
                    others = [lax.rem(z + d, 4) for d in (1, 2, 3)]
                else:
                    others = [1 - self.here[order[k]]]
                for i, (other, peer) in enumerate(zip(others, peers[order[k]])):
                    index = [other if d == order[k] else slice(None) for d in held_after(order, k)]
                    target = got[k].at[i] if order[k] == "z" else got[k]
                    self.groups[k + 1].append(
                        remote(source.at[(*index, *cut)], target, sems, slot, peer)
                    )
                    slot += 1

    @staticmethod
    def shapes(r, n, mine, orders=FIRST_Z):
        result = [VMEM((4, 2, 2, r, n), BF16)] * (2 if mine else 1)
        for (low, high), order in zip(halves(0, n), orders):
            order = order[::-1]
            for k in range(3):
                held = [SIZES[d] for d in held_after(order, k + 1)]
                lead = [3] if order[k] == "z" else []
                result.append(VMEM((*lead, *held, r, high - low), BF16))
        return result

    def add(self, lane, k):
        cols, order, got = lane
        before = held_after(order, k)
        after = held_after(order, k + 1)

        def total(index):
            at = dict(zip(after, index))
            at[order[k]] = self.here[order[k]]
            where = tuple(at[d] for d in before)
            if k == 0:
                value = self.one[(*where, slice(None), cols)]
            else:
                lead = (0,) if order[k - 1] == "z" else ()
                value = got[k - 1][(*lead, *where)]
            lead = [(i,) for i in range(3)] if order[k] == "z" else [()]
            if k == 2:
                value = value.astype(F32)
                for i in lead:
                    value = value + got[k][i + index].astype(F32)
                return value
            for i in lead:
                value = value + got[k][i + index]
            got[k][lead[0] + index] = value

        if not after:
            return total(())
        sizes = [SIZES[d] for d in after]

        def loop(i, carry):
            if len(sizes) == 1:
                total((i,))
            else:
                for j in range(sizes[1]):
                    total((i, j))
            return carry

        lax.fori_loop(0, sizes[0], loop, 0)

    def run(self, stage):
        if stage == 0 and self.mine is not None:
            self.kept.start()
        if stage == 1 and self.mine is not None:
            self.kept.wait()
        if 1 <= stage <= 4:
            for copy in self.groups[stage - 1]:
                copy.wait_recv()
        if stage == 1:

            def add(i, carry):
                a, b = i // 2, i % 2
                own = self.grads[a, b, self.core_at] if self.mine is None else self.mine[a, b]
                self.one[a, b] = self.one[a, b] + own
                return carry

            lax.fori_loop(0, 8, add, 0)
        if stage in (2, 3):
            for lane in self.lanes:
                self.add(lane, stage - 2)
        if stage == 4:
            values = [self.add(lane, 2) for lane in self.lanes]
            self.put(values[0] if len(values) == 1 else jnp.concatenate(values, axis=1))
        if stage <= 3:
            for copy in self.groups[stage]:
                copy.start()
        if stage == 5:
            for copies in self.groups:
                for copy in copies:
                    copy.wait_send()


def fold(values, each, row):
    width = 32 * each
    shard = lax.broadcasted_iota(jnp.int32, (32, 16, width), 0)
    col = lax.broadcasted_iota(jnp.int32, (32, 16, width), 2)
    inside = (col >= shard * each) & (col < shard * each + each)
    spreaded = jnp.where(inside, values[None], 0.0).reshape(32 * 16, width).astype(BF16)
    lane = lax.broadcasted_iota(jnp.int32, (128, width), 0)
    col = lax.broadcasted_iota(jnp.int32, (128, width), 1)
    return nt(spreaded, (lax.rem(col, each) == lane).astype(BF16))


BACKWARD = {
    "h": ("D0", "E0", "U0",),
    0: ("V0", "O0",),
    1: ("D1",),
    5: ("E1",),
    6: ("D2",),
    "g0": ("X0", "U1",),
    10: ("V1",),
    12: ("E2",),
    14: ("D3", "U2",),
    "g1": ("V2", "Y0",),
    17: ("O1", "U3",),
    18: ("X1",),
    20: ("E3",),
    21: ("V3", "O2", "X2",),
    22: ("Y1",),
    23: ("O3",),
    "t0": ("Z0",),
    "t1": ("X3", "Y2", "Z1",),
    "t3": ("Y3",),
    "f": ("Z2",),
    "e": ("S0",),
    "last": ("S1", "Z3", "S2", "S3", "D4", "E4", "U4", "V4", "O4", "X4", "Y4", "Z4", "S4",),
}
GROUPS = 3


def scatter_backward_kernel(
    x_all, dy1_all, vec24_ref, wqkv_all, qkv_all, o_all, do_all, lse_ref, s24_mid, s96_mid,
    gout_all, gup_all, gdown_all,
    gx_ref, gqkv_ref, gout_ref, gup_ref, gdown_ref, small_ref,
    dqkv, h1_t, kt, dk, dv, s24_ref, s72_ref, small_all,
    x_ref, qkv_ref, do_ref, o_ref, dy1_ref, wqkv_ref, *buffers,
):
    send, recv, local, load = buffers[-4:]
    buffers = list(buffers[:-4])
    greet()
    inputs = (
        (x_all, x_ref), (qkv_all, qkv_ref), (do_all, do_ref), (o_all, o_ref), (dy1_all, dy1_ref),
        (wqkv_all, wqkv_ref),
    )
    loads = [pltpu.make_async_copy(a, b, load.at[i]) for i, (a, b) in enumerate(inputs)]
    half = gdown_all.shape[-2] // 2
    parts = {}

    def add_part(name, grads, mine, put, **view):
        i = len(parts)
        held = [buffers.pop(0)] if mine else [None]
        count = 4 if len(halves(0, grads.shape[-1])) == 1 else 7
        held += [buffers.pop(0) for _ in range(count)]
        parts[name] = Scatter(grads, held, (send.at[i], recv.at[i]), local.at[i], put, **view)

    def put_at(ref, rows, cols):
        def put(value):
            ref[rows, cols] = value

        return put

    every = slice(None)
    for name, k in (("U", 0), ("V", 1)):
        cols = (k * FF // 2, (k + 1) * FF // 2)
        add_part(name, gup_all, True, put_at(gup_ref, every, slice(*cols)), cols=cols, orders=UP_ORDERS)
    for name, k in (("D", 0), ("E", 1)):
        rows = (k * half, (k + 1) * half)
        add_part(name, gdown_all, True, put_at(gdown_ref, slice(*rows), every), rows=rows, orders=DOWN_ORDERS)
    add_part("O", gout_all, True, put_at(gout_ref, every, every))
    groups = [buffers.pop(0) for _ in range(GROUPS)]

    def put_group(group):
        def put(value):
            for part in range(3):
                low = part * D + group * 256
                gqkv_ref[:, low : low + 256] = value[:, part * 256 : (part + 1) * 256]

        return put

    for group, name in enumerate("XYZ"):
        add_part(name, groups[group], False, put_group(group))
    add_part("S", small_all, False, put_at(small_ref, every, every))

    run = runner(parts, BACKWARD)
    run("h")
    for copy in loads:
        copy.start()
    s24_ref[...] = jnp.zeros_like(s24_ref)
    s72_ref[...] = jnp.zeros_like(s72_ref)
    length = x_ref.shape[0]
    steps = length // BLK

    def hidden_rows(block, carry):
        here = pl.ds(pl.multiple_of(block * BLK, BLK), BLK)
        normed, _ = norm_parts(x_ref[here, :].astype(F32))
        hidden = (normed * vec24_ref[0:1, :] + vec24_ref[1:2, :]).astype(BF16)
        h1_t[:, here] = hidden.T
        return carry

    loads[0].wait()
    lax.fori_loop(0, steps, hidden_rows, 0)
    for copy in loads[1:4]:
        copy.wait()

    def group_grads(group):
        def one(i, carry):
            left = pl.ds(pl.multiple_of(i * (D // 4), D // 4), D // 4)
            for part in range(3):
                low = part * D + group * 256
                value = nn(h1_t[left, :], dqkv[:, low : low + 256])
                value = value.reshape(2, 2, 2, D // 32, 256).astype(BF16)
                groups[group][i, :, :, :, :, part * 256 : (part + 1) * 256] = value
            return carry

        lax.fori_loop(0, 4, one, 0)

    def one(pair, carry):
        def event(j):
            at_step = steps - 1 - j
            if at_step == 0:
                for group in range(GROUPS - 1):

                    @pl.when(pair == 2 * group + 2)
                    def _():
                        group_grads(group)
                        run(f"g{group}")

            spots = [(p, p * steps + at_step) for p in range(HEADS // 2)]
            when_run(run, BACKWARD, pair, spots)

        attention_back_pair(pair, qkv_ref, o_ref, do_ref, lse_ref, dqkv, kt, dk, dv, event)
        return carry

    lax.fori_loop(0, HEADS // 2, one, 0)
    run("g2")
    group_grads(GROUPS - 1)
    for copy in loads[4:]:
        copy.wait()

    def tail(block, carry):
        when_run(run, BACKWARD, block, [(b, f"t{b}") for b in range(steps)])
        tail_rows(block, x_ref, dy1_ref, vec24_ref, wqkv_ref, dqkv, None, gx_ref, s24_ref, s72_ref)
        return carry

    lax.fori_loop(0, steps, tail, 0)
    run("f")
    total = fold(s24_ref[...] + s24_mid[...], 24, 0)
    total = total + fold(s72_ref[...], 72, 6) + fold(s96_mid[...], 96, 7)
    small_all[...] = total.reshape(4, 2, 2, 2, 16, 128).astype(BF16)
    run("e")
    run("last")
    for part in parts.values():
        part.run(5)


def scatter_backward_call(
    x, dy1, vec24, wqkv, qkv, attended, grad_attended, lse, s24, s96, gout, gup, gdown
):
    length = x.shape[0]
    anywhere = pl.BlockSpec(memory_space=pl.ANY)
    inside = pl.BlockSpec(memory_space=VMEM)
    deep = gdown.shape[-2]
    scratch = [
        VMEM((length, 3 * D), BF16),
        VMEM((D, length), BF16),
        VMEM((128, length), BF16),
        VMEM((length, 128), F32),
        VMEM((length, 128), F32),
        VMEM((16, D), F32),
        VMEM((16, 3 * D), F32),
        VMEM((4, 2, 2, 2, 16, 128), BF16),
        VMEM((length, D), BF16),
        VMEM((length, 3 * D), BF16),
        VMEM((length, D), BF16),
        VMEM((length, D), BF16),
        VMEM((length, D), F32),
        VMEM((D, 3 * D), BF16),
    ]
    for _ in range(2):
        scratch += Scatter.shapes(D // 32, FF // 2, True, UP_ORDERS)
    for _ in range(2):
        scratch += Scatter.shapes(deep // 2, D, True, DOWN_ORDERS)
    scratch += Scatter.shapes(D // 32, D, True)
    scratch += [VMEM((4, 2, 2, 2, D // 32, D), BF16)] * GROUPS
    for _ in range(GROUPS):
        scratch += Scatter.shapes(D // 32, D, False)
    scratch += Scatter.shapes(16, 128, False)
    scratch += [pltpu.SemaphoreType.DMA((9, Scatter.slots))] * 2 + [pltpu.SemaphoreType.DMA((9,))]
    scratch += [pltpu.SemaphoreType.DMA((6,))]
    return pl.pallas_call(
        scatter_backward_kernel,
        out_shape=(
            jax.ShapeDtypeStruct((length, D), BF16),
            jax.ShapeDtypeStruct((D // 32, 3 * D), F32),
            jax.ShapeDtypeStruct((D // 32, D), F32),
            jax.ShapeDtypeStruct((D // 32, FF), F32),
            jax.ShapeDtypeStruct((deep, D), F32),
            jax.ShapeDtypeStruct((16, 128), F32),
        ),
        in_specs=[
            anywhere, anywhere, inside, *[anywhere] * 4, inside, inside, inside, *[anywhere] * 3
        ],
        out_specs=(inside,) * 6,
        scratch_shapes=scratch,
        compiler_params=pltpu.CompilerParams(
            collective_id=2, has_side_effects=True, vmem_limit_bytes=63 * 2**20
        ),
    )(x, dy1, vec24, wqkv, qkv, attended, grad_attended, lse, s24, s96, gout, gup, gdown)


def shards(
    tokens, cotangent, lengths, ln1_gain, ln1_shift, qkv_weight, qkv_bias, out_weight, out_bias,
    ln2_gain, ln2_shift, up_weight, up_bias, down_weight, down_bias, *, special,
):
    vectors = (ln1_gain, ln1_shift, out_bias, ln2_gain, ln2_shift, down_bias, qkv_bias, up_bias)
    if special:
        small = jnp.stack(
            [jnp.pad(v, (0, 128 - v.shape[0])) for v in vectors] + [jnp.zeros((128,), BF16)] * 8
        )
        wqkv, wout, wup, wdown, vec24, vec96, qkv, attended, lse = gather_forward_call(
            tokens, small, qkv_weight, out_weight, up_weight, down_weight
        )
        wout, wup = (w.reshape(D, w.shape[-1]) for w in (wout, wup))
        wdown = wdown.reshape(FF, D)
    else:
        gather = functools.partial(lax.all_gather, axis_name=AXES, axis=0, tiled=True)
        wqkv, wout, wup, wdown = map(gather, (qkv_weight, out_weight, up_weight, down_weight))
        whole = [gather(v).astype(F32) for v in vectors]
        vec24 = jnp.pad(jnp.stack(whole[:6]), ((0, 10), (0, 0)))
        vec72 = jnp.pad(whole[6][None], ((6, 9), (0, 0)))
        vec96 = jnp.pad(whole[7][None], ((7, 8), (0, 0)))
        qkv, attended, lse = forward_call(tokens, vec24, vec72, wqkv)
    mixed, do, dy1, gout, gup, gdown, s24_mid, s96 = middle_call(
        lengths, tokens, attended, cotangent, vec24, vec96, wout, wup, wdown, 32
    )
    if special:
        gout, gup = (g.reshape(4, 2, 2, 2, *g.shape[1:]) for g in (gout, gup))
        gdown = gdown.reshape(4, 2, 2, 2, FF // 32, D)
        gx, gqkv, gout, gup, gdown, small = scatter_backward_call(
            tokens, dy1, vec24, wqkv, qkv, attended, do, lse, s24_mid, s96, gout, gup, gdown
        )
        sizes = [v.shape[0] for v in vectors]
        folded = [small[i, :n] for i, n in enumerate(sizes)]
    else:
        gx, gqkv, s24, s72 = backward_call(tokens, dy1, vec24, wqkv, qkv, attended, do, lse, 32)
        scatter = functools.partial(
            lax.psum_scatter, axis_name=AXES, scatter_dimension=0, tiled=True
        )
        gqkv, gout, gup = (scatter(g.reshape(D, -1).astype(F32)) for g in (gqkv, gout, gup))
        gdown = scatter(gdown.reshape(FF, D).astype(F32))
        both = s24 + s24_mid
        folded = [scatter(both[i]) for i in range(6)] + [scatter(s72[6]), scatter(s96[7])]
    return (
        mixed, gx, folded[0], folded[1], gqkv, folded[6], gout, folded[2], folded[3], folded[4],
        gup, folded[7], gdown, folded[5],
    )


def solution(mesh):
    flat, rows = P(AXES), P(AXES, None)
    in_specs = (
        rows, rows, flat, flat, flat, rows, flat, rows, flat, flat, flat, rows, flat, rows, flat,
    )
    out_specs = (
        rows, rows, flat, flat, rows, flat, rows, flat, flat, flat, rows, flat, rows, flat,
    )
    special = dict(mesh.shape) == {"wide": 16, "narrow": 2}
    return jax.shard_map(
        functools.partial(shards, special=special),
        mesh=mesh, in_specs=in_specs, out_specs=out_specs, check_vma=False,
    )
```

time: 366 us -> 228 us (0.62)
  Pallas kernels: 341 us -> 213 us
  local copies, waits for them, and re-layouts: 23.6 us -> 13.2 us
    pallas_call x5 -> x3, Pallas kernels: 341 us -> 213 us  [the longest x1 85.7 us: scatter_backward_call(): pl.pallas_call(scatter_backward_kernel, out_shape=(jax.ShapeDtypeStruct((...]
    unnamed x24 -> x13, local copies, waits for them, and re-layouts: 17 us -> 5.49 us
where the time goes in v2:
time: 228 us; the launch traced here: 227 us
  Pallas kernels  213 us (93%)
  local copies, waits for them, and re-layouts  13.2 us (6%)
    pallas_call x1, Pallas kernels, scatter_backward_call(): pl.pallas_call(scatter_backward_kernel, out_shape=(jax.ShapeDtypeStruct((...  85.7 us
    pallas_call x1, Pallas kernels, gather_forward_call(): pl.pallas_call(gather_forward_kernel, out_shape=(jax.ShapeDtypeStruct((D,...  75.5 us
    pallas_call x1, Pallas kernels, middle_call(): pl.pallas_call(middle_kernel, grid=(length // MID,), out_shape=tuple((jax...  51.5 us
    unnamed x13, local copies, waits for them, and re-layouts  5.49 us

profile of v2, /device:TPU:0, one launch (start us, length us, event | category | flops | bytes accessed | tf_op | source)
XLA Modules:
  0.0 227.3 jit_solution(2653082698286642514)
XLA Ops:
  1.3 0.7 pad_bitcast_fusion.6
  2.0 0.7 pad_bitcast_fusion
  2.6 0.7 pad_bitcast_fusion.4
  3.3 0.7 pad_bitcast_fusion.2
  4.0 1.2 stack.39.small_ref
  5.2 75.5 %shard_map.254 = (bf16[768,2304]{1,0:T(8,128)(2,1)}, bf16[4,2,2,2,24,768]{5,4,3,2,1,0:T(8,128)(2,1)}, bf16[4,2,2,2,24,3072]{5,4,3,2,1,0:T(8,128)(2,1)}, bf16[4,2...) custom-call(bf16[1024,768]{1,0:T(8,128)(2,1)} %x_all.1, ...), custom_call_target="tpu_custom_call" | custom-call | tf_op jit(solution)/shard_map/pallas_call | solution.py:682
  80.7 51.5 %shard_map.255 = (bf16[1024,768]{1,0:T(8,128)(2,1)}, bf16[1024,768]{1,0:T(8,128)(2,1)}, f32[1024,768]{1,0:T(8,128)}, bf16[32,24,768]{2,1,0:T(8,128)(2,1)}, bf16[...) custom-call(s32[1]{0:T(128)S(6)} %copy.34.len_ref, ...), custom_call_target="tpu_custom_call" | custom-call | tf_op jit(solution)/shard_map/pallas_call | solution.py:314
  132.3 85.7 %shard_map.256 = (bf16[1024,768]{1,0:T(8,128)(2,1)}, f32[24,2304]{1,0:T(8,128)}, f32[24,768]{1,0:T(8,128)}, f32[24,3072]{1,0:T(8,128)}, f32[96,768]{1,0:T(8,128)}, /*index=5*/f32[16,128]{1,0:T(8,128)}) custom-call(bf16[1024,768]{1,0:T(8,128)(2,1)} %x_all.1, f32[1024,768]{1,0:T(8,128)} %get-tuple-element.44.dy1_all, f32[16,768]{1,0:T(8,128)} %get-tuple-element.38.vec24_ref, ...), custom_call_target="tpu_custom_call" | custom-call | tf_op jit(solution)/shard_map/pallas_call | solution.py:1042
  218.0 1.2 slice_bitcast_fusion.5
  219.2 1.2 slice_bitcast_fusion.1
  220.4 1.4 slice_bitcast_fusion
  221.8 0.0 copy-start.2
  221.8 0.0 copy-start.3
  221.8 0.0 copy-start.1
  221.8 0.0 copy-start
  221.8 2.7 %copy.35 = bf16[1024,768]{1,0:T(8,128)(2,1)} copy(bf16[1024,768]{1,0:T(8,128)(2,1)} %get-tuple-element.89) | data formatting | bytes 3145728
  224.5 0.0 copy-done.2
  224.5 0.7 copy.36
  225.2 0.0 copy-done.3
  225.2 0.6 copy.37
  225.9 0.0 copy-done.1
  225.9 0.7 copy.38
  226.6 0.0 copy-done
  226.6 0.7 copy.39
  (1 shorter events, 0.0 us)
Async XLA Ops:
  221.8 2.8 %copy-start.2 = (f32[24,2304]{1,0:T(8,128)S(1)}, f32[24,2304]{1,0:T(8,128)}, u32[]{:S(2)}) copy-start(f32[24,2304]{1,0:T(8,128)} %get-tuple-element.92) | copy-start | bytes 663556
  221.8 3.4 %copy-start.3 = (f32[24,768]{1,0:T(8,128)S(1)}, f32[24,768]{1,0:T(8,128)}, u32[]{:S(2)}) copy-start(f32[24,768]{1,0:T(8,128)} %get-tuple-element.94) | copy-start | bytes 221188
  221.8 4.1 %copy-start.1 = (f32[24,3072]{1,0:T(8,128)S(1)}, f32[24,3072]{1,0:T(8,128)}, u32[]{:S(2)}) copy-start(f32[24,3072]{1,0:T(8,128)} %get-tuple-element.98) | copy-start | bytes 884740
  221.8 4.8 %copy-start = (f32[96,768]{1,0:T(8,128)S(1)}, f32[96,768]{1,0:T(8,128)}, u32[]{:S(2)}) copy-start(f32[96,768]{1,0:T(8,128)} %get-tuple-element.100) | copy-start | bytes 884740

commit v3 on v2

--- a/solution.py
+++ b/solution.py
@@ -1060,6 +1060,37 @@
     )(x, dy1, vec24, wqkv, qkv, attended, grad_attended, lse, s24, s96, gout, gup, gdown)
 
 
+def finish_kernel(
+    gx, gqkv, gout, gup, gdown, small, gx_out, gqkv_out, gout_out, gup_out, gdown_out, *vectors
+):
+    gx_out[...] = gx[...]
+    gqkv_out[...] = gqkv[...]
+    gout_out[...] = gout[...]
+    gup_out[...] = gup[...]
+    gdown_out[...] = gdown[...]
+    for row, out in enumerate(vectors):
+        out[...] = small[row, 0 : out.shape[0]]
+
+
+def finish_call(mixed, gx, gqkv, gout, gup, gdown, small, shapes):
+    inside = pl.BlockSpec(memory_space=VMEM)
+    whole = (gqkv, gout, gup, gdown)
+    outs = [jax.ShapeDtypeStruct(gx.shape, gx.dtype)]
+    outs += [jax.ShapeDtypeStruct(a.shape, F32) for a in whole]
+    outs += [jax.ShapeDtypeStruct(shape, F32) for shape in shapes]
+    gx, gqkv, gout, gup, gdown, *folded = pl.pallas_call(
+        finish_kernel,
+        out_shape=tuple(outs),
+        in_specs=[inside] * 6,
+        out_specs=(inside,) * len(outs),
+        compiler_params=pltpu.CompilerParams(vmem_limit_bytes=60 * 2**20),
+    )(gx, *whole, small)
+    return (
+        mixed, gx, folded[0], folded[1], gqkv, folded[6], gout, folded[2], folded[3], folded[4],
+        gup, folded[7], gdown, folded[5],
+    )
+
+
 def shards(
     tokens, cotangent, lengths, ln1_gain, ln1_shift, qkv_weight, qkv_bias, out_weight, out_bias,
     ln2_gain, ln2_shift, up_weight, up_bias, down_weight, down_bias, *, special,
@@ -1091,8 +1122,7 @@
         gx, gqkv, gout, gup, gdown, small = scatter_backward_call(
             tokens, dy1, vec24, wqkv, qkv, attended, do, lse, s24_mid, s96, gout, gup, gdown
         )
-        sizes = [v.shape[0] for v in vectors]
-        folded = [small[i, :n] for i, n in enumerate(sizes)]
+        return finish_call(mixed, gx, gqkv, gout, gup, gdown, small, [v.shape for v in vectors])
     else:
         gx, gqkv, s24, s72 = backward_call(tokens, dy1, vec24, wqkv, qkv, attended, do, lse, 32)
         scatter = functools.partial(

time: 228 us -> 222 us (0.974)
  local copies, waits for them, and re-layouts: 13.2 us -> 3.9 us
  Pallas kernels: 213 us -> 216 us
    unnamed x13 -> x0, local copies, waits for them, and re-layouts: 5.49 us -> none
    squeeze x3 -> x0, local copies, waits for them, and re-layouts: 3.8 us -> none  [shards(): folded = [small[i, :n] for i, n in enumerate(sizes)]]
    pallas_call x0 -> x1, Pallas kernels: none -> 3.12 us  [finish_call(): pl.pallas_call(finish_kernel, out_shape=tuple(outs), in_specs=[inside] *...]
where the time goes in v3:
time: 222 us; the launch traced here: 221 us
  Pallas kernels  216 us (97%)
  local copies, waits for them, and re-layouts  3.9 us (2%)
    pallas_call x1, Pallas kernels, scatter_backward_call(): pl.pallas_call(scatter_backward_kernel, out_shape=(jax.ShapeDtypeStruct((...  85.7 us
    pallas_call x1, Pallas kernels, gather_forward_call(): pl.pallas_call(gather_forward_kernel, out_shape=(jax.ShapeDtypeStruct((D,...  75.6 us
    pallas_call x1, Pallas kernels, middle_call(): pl.pallas_call(middle_kernel, grid=(length // MID,), out_shape=tuple((jax...  51.6 us

profile of v3, /device:TPU:0, one launch (start us, length us, event | category | flops | bytes accessed | tf_op | source)
XLA Modules:
  0.0 221.4 jit_solution(11252794519516177991)
XLA Ops:
  1.3 0.7 pad_bitcast_fusion.6
  2.0 0.7 pad_bitcast_fusion
  2.6 0.7 pad_bitcast_fusion.4
  3.3 0.7 pad_bitcast_fusion.2
  4.0 1.2 stack.39.small_ref
  5.2 75.6 %shard_map.254 = (bf16[768,2304]{1,0:T(8,128)(2,1)}, bf16[4,2,2,2,24,768]{5,4,3,2,1,0:T(8,128)(2,1)}, bf16[4,2,2,2,24,3072]{5,4,3,2,1,0:T(8,128)(2,1)}, bf16[4,2...) custom-call(bf16[1024,768]{1,0:T(8,128)(2,1)} %x_all.1, ...), custom_call_target="tpu_custom_call" | custom-call | tf_op jit(solution)/shard_map/pallas_call | solution.py:682
  80.8 51.6 %shard_map.255 = (bf16[1024,768]{1,0:T(8,128)(2,1)}, bf16[1024,768]{1,0:T(8,128)(2,1)}, f32[1024,768]{1,0:T(8,128)}, bf16[32,24,768]{2,1,0:T(8,128)(2,1)}, bf16[...) custom-call(s32[1]{0:T(128)S(6)} %copy.29.len_ref, ...), custom_call_target="tpu_custom_call" | custom-call | tf_op jit(solution)/shard_map/pallas_call | solution.py:314
  132.4 85.7 %shard_map.256 = (bf16[1024,768]{1,0:T(8,128)(2,1)}, f32[24,2304]{1,0:T(8,128)}, f32[24,768]{1,0:T(8,128)}, f32[24,3072]{1,0:T(8,128)}, f32[96,768]{1,0:T(8,128)}, /*index=5*/f32[16,128]{1,0:T(8,128)}) custom-call(bf16[1024,768]{1,0:T(8,128)(2,1)} %x_all.1, f32[1024,768]{1,0:T(8,128)} %get-tuple-element.57.dy1_all, f32[16,768]{1,0:T(8,128)} %get-tuple-element.51.vec24_ref, ...), custom_call_target="tpu_custom_call" | custom-call | tf_op jit(solution)/shard_map/pallas_call | solution.py:1042
  218.1 3.1 %shard_map.257 = (bf16[1024,768]{1,0:T(8,128)(2,1)}, f32[24,2304]{1,0:T(8,128)}, f32[24,768]{1,0:T(8,128)}, f32[24,3072]{1,0:T(8,128)}, f32[96,768]{1,0:T(8,128)...) custom-call(bf16[1024,768]{1,0:T(8,128)(2,1)} %get-tuple-element.67., ...), custom_call_target="tpu_custom_call" | custom-call | tf_op jit(solution)/shard_map/pallas_call | solution.py:1081
  (1 shorter events, 0.0 us)

commit v4 on v3

--- a/solution.py
+++ b/solution.py
@@ -1060,6 +1060,25 @@
     )(x, dy1, vec24, wqkv, qkv, attended, grad_attended, lse, s24, s96, gout, gup, gdown)
 
 
+def pack_kernel(*refs):
+    *vectors, out, rows = refs
+    rows[...] = jnp.zeros_like(rows)
+    for row, vector in enumerate(vectors):
+        rows[row, 0 : vector.shape[0]] = vector[...].astype(F32)
+    out[...] = rows[...].astype(BF16)
+
+
+def pack_call(vectors):
+    inside = pl.BlockSpec(memory_space=VMEM)
+    return pl.pallas_call(
+        pack_kernel,
+        out_shape=jax.ShapeDtypeStruct((16, 128), BF16),
+        in_specs=[inside] * len(vectors),
+        out_specs=inside,
+        scratch_shapes=[VMEM((16, 128), F32)],
+    )(*vectors)
+
+
 def finish_kernel(
     gx, gqkv, gout, gup, gdown, small, gx_out, gqkv_out, gout_out, gup_out, gdown_out, *vectors
 ):
@@ -1097,9 +1116,7 @@
 ):
     vectors = (ln1_gain, ln1_shift, out_bias, ln2_gain, ln2_shift, down_bias, qkv_bias, up_bias)
     if special:
-        small = jnp.stack(
-            [jnp.pad(v, (0, 128 - v.shape[0])) for v in vectors] + [jnp.zeros((128,), BF16)] * 8
-        )
+        small = pack_call(vectors)
         wqkv, wout, wup, wdown, vec24, vec96, qkv, attended, lse = gather_forward_call(
             tokens, small, qkv_weight, out_weight, up_weight, down_weight
         )

time: 222 us -> 219 us (0.986)
  local copies, waits for them, and re-layouts: 3.9 us -> 0 us
    another operation x6 -> x0, local copies, waits for them, and re-layouts: 3.9 us -> none  [shards(): jnp.stack([jnp.pad(v, (0, 128 - v.shape[0])) for v in vectors] + [jnp.zer...]
where the time goes in v4:
time: 219 us
  Pallas kernels  217 us (99%)
    pallas_call x1, Pallas kernels, scatter_backward_call(): pl.pallas_call(scatter_backward_kernel, out_shape=(jax.ShapeDtypeStruct((...  85.7 us
    pallas_call x1, Pallas kernels, gather_forward_call(): pl.pallas_call(gather_forward_kernel, out_shape=(jax.ShapeDtypeStruct((D,...  75.5 us
    pallas_call x1, Pallas kernels, middle_call(): pl.pallas_call(middle_kernel, grid=(length // MID,), out_shape=tuple((jax...  51.5 us

profile of v4, /device:TPU:0, one launch (start us, length us, event | category | flops | bytes accessed | tf_op | source)
XLA Modules:
  0.0 218.8 jit_solution(725061372861983446)
XLA Ops:
  1.3 1.4 shard_map.254.small_ref
  2.7 75.5 %shard_map.255 = (bf16[768,2304]{1,0:T(8,128)(2,1)}, bf16[4,2,2,2,24,768]{5,4,3,2,1,0:T(8,128)(2,1)}, bf16[4,2,2,2,24,3072]{5,4,3,2,1,0:T(8,128)(2,1)}, bf16[4,2...) custom-call(bf16[1024,768]{1,0:T(8,128)(2,1)} %x_all.1, ...), custom_call_target="tpu_custom_call" | custom-call | tf_op jit(solution)/shard_map/pallas_call | solution.py:682
  78.2 51.5 %shard_map.256 = (bf16[1024,768]{1,0:T(8,128)(2,1)}, bf16[1024,768]{1,0:T(8,128)(2,1)}, f32[1024,768]{1,0:T(8,128)}, bf16[32,24,768]{2,1,0:T(8,128)(2,1)}, bf16[...) custom-call(s32[1]{0:T(128)S(6)} %copy.29.len_ref, ...), custom_call_target="tpu_custom_call" | custom-call | tf_op jit(solution)/shard_map/pallas_call | solution.py:314
  129.8 85.7 %shard_map.257 = (bf16[1024,768]{1,0:T(8,128)(2,1)}, f32[24,2304]{1,0:T(8,128)}, f32[24,768]{1,0:T(8,128)}, f32[24,3072]{1,0:T(8,128)}, f32[96,768]{1,0:T(8,128)}, /*index=5*/f32[16,128]{1,0:T(8,128)}) custom-call(bf16[1024,768]{1,0:T(8,128)(2,1)} %x_all.1, f32[1024,768]{1,0:T(8,128)} %get-tuple-element.57.dy1_all, f32[16,768]{1,0:T(8,128)} %get-tuple-element.51.vec24_ref, ...), custom_call_target="tpu_custom_call" | custom-call | tf_op jit(solution)/shard_map/pallas_call | solution.py:1042
  215.5 3.1 %shard_map.258 = (bf16[1024,768]{1,0:T(8,128)(2,1)}, f32[24,2304]{1,0:T(8,128)}, f32[24,768]{1,0:T(8,128)}, f32[24,3072]{1,0:T(8,128)}, f32[96,768]{1,0:T(8,128)...) custom-call(bf16[1024,768]{1,0:T(8,128)(2,1)} %get-tuple-element.67., ...), custom_call_target="tpu_custom_call" | custom-call | tf_op jit(solution)/shard_map/pallas_call | solution.py:1100
